TPU v7x, 128 devices: a whole 4x4x4 slice. The times are simulated.
128 devices in a mesh: clip: 4 (over y), tm: 32 (over x, z, core).
Axes of the slice: x: 4, y: 4, z: 4, core: 2. Of those that a mesh axis runs over, the one named last changes fastest.
Arguments:
- latent: bfloat16 [8, 512, 64], P('clip', 'tm'), may hold values from -6 to 6
- dest: int32 [8], replicated, may hold values from 0 to 7, each once
- lengths: int32 [8], replicated, may hold values from 128 to 512, as said below
- input_conv_weight: bfloat16 [7, 64, 2048], replicated, may hold values from -0.25 to 0.25
- snake_entry_frequency: float32 [2048], replicated, may hold values from 0.5 to 2
- upsample_weight: bfloat16 [2048, 16, 1024], P('tm', None, 'clip'), may hold values from -0.09375 to 0.09375
- snake_unit_frequency: float32 [2, 2, 1024], P(None, None, 'clip'), may hold values from 0.5 to 2
- dilated_conv_weight: bfloat16 [2, 7, 1024, 1024], P(None, None, 'tm', 'clip'), may hold values from -0.0625 to 0.0625
- pointwise_conv_weight: bfloat16 [2, 1024, 1024], P(None, 'tm', 'clip'), may hold values from -0.1875 to 0.1875
Outputs:
- decoded: bfloat16 [8, 4096, 1024], P(None, 'tm', 'clip')
- energy: float32 [8, 1024], P(None, ('clip', 'tm'))
Inputs may be any that keep to these rules, and one draw needn't show every extreme that they name: `lengths`: at least one slot has all 512 frames live; no slot has fewer than 128.
All inputs are finite; a program needn't handle non-finite values.
Results may differ from a plain program's by a relative error of at most 0.012.
Values may be sent and summed in bfloat16 or wider, within the bound.
No kernel may reach another device: no remote copies, remote signals or barrier semaphores. Data moves between devices by JAX's collectives and lax.ppermute only.
A program may use at most 128 MiB of HBM per device.

v0:
```python
import jax
import jax.numpy as jnp
from jax import lax
from jax.sharding import PartitionSpec as P


def padded(block, sides, width):
    for axis, dim in sides:
        count = lax.axis_size(axis)
        forward = [(i, i + 1) for i in range(count - 1)]
        backward = [(target, source) for source, target in forward]
        low = lax.ppermute(
            lax.slice_in_dim(block, block.shape[dim] - width, None, axis=dim), axis, forward
        )
        high = lax.ppermute(lax.slice_in_dim(block, 0, width, axis=dim), axis, backward)
        block = jnp.concatenate([low, block, high], axis=dim)
    return block


def snake(value, alpha):
    return value + jnp.sin(alpha * value) ** 2 / alpha


def kernel_tap_count(source_signal, weight_bundle, dilation_factor, signal_length):
    total = None
    for kernel_tap in range(weight_bundle.shape[0]):
        replay_window = lax.slice_in_dim(
            source_signal,
            kernel_tap * dilation_factor,
            kernel_tap * dilation_factor + signal_length,
            axis=1,
        )
        term = jnp.einsum(
            "cli,io->clo",
            replay_window,
            weight_bundle[kernel_tap],
            preferred_element_type=jnp.float32,
        )
        total = term if total is None else total + term
    return total


def widen(value):
    return lax.all_gather(value, "clip", axis=2, tiled=True)


def body(
    latent,
    dest,
    lengths,
    input_conv_weight,
    snake_entry_frequency,
    upsample_weight,
    snake_unit_frequency,
    dilated_conv_weight,
    pointwise_conv_weight,
):
    frames = latent.shape[1]
    tm_index = lax.axis_index("tm")
    upk = upsample_weight.shape[1]
    c1_local = upsample_weight.shape[2]
    quarter = upk // 4
    stride = upk // 2
    sample_rows = stride * frames
    residual_unit_list = dilated_conv_weight.shape[0]
    gathered = lax.all_gather(latent, "clip", axis=0, tiled=True)
    picked = jnp.take(gathered, dest, axis=0)
    frame_pos = tm_index * frames + jnp.arange(frames)
    live = frame_pos[None, :] < lengths[:, None]
    picked = jnp.where(live[:, :, None], picked, jnp.zeros_like(picked))
    extended = padded(picked, (("tm", 1),), 3)
    pre = kernel_tap_count(extended, input_conv_weight, 1, frames)
    s_core = snake(pre, snake_entry_frequency).astype(jnp.bfloat16)
    s_zero = padded(s_core, (("tm", 1),), 1)
    clips = s_zero.shape[0]
    span = s_zero.shape[1]
    flat = s_zero.reshape(clips * span, s_zero.shape[2])
    add_piece = lax.all_gather(upsample_weight, "tm", axis=0, tiled=True)
    rows = add_piece.shape[0]
    prod = jnp.dot(
        flat, add_piece.reshape(rows, upk * c1_local), preferred_element_type=jnp.float32
    )
    prod = prod.reshape(clips, span, upk, c1_local)
    first = prod[:, 1:-1, quarter : 2 * quarter] + prod[:, :-2, 3 * quarter : 4 * quarter]
    second = prod[:, 1:-1, 2 * quarter : 3 * quarter] + prod[:, 2:, 0:quarter]
    state = jnp.concatenate([first, second], axis=2).reshape(clips, (span - 2) * stride, c1_local)
    for residual_unit in range(residual_unit_list):
        dilation_factor = 3**residual_unit
        receptive_reach = 3 * dilation_factor
        signal_length = state.shape[1]
        snake_activation = snake(state, snake_unit_frequency[residual_unit, 0])
        snake_activation = padded(
            snake_activation.astype(jnp.bfloat16), (("tm", 1),), receptive_reach
        )
        widened_signal = widen(snake_activation)
        inner_signal = kernel_tap_count(
            widened_signal,
            lax.all_gather(dilated_conv_weight[residual_unit], "tm", axis=1, tiled=True),
            dilation_factor,
            signal_length,
        )
        branch = widen(
            snake(inner_signal, snake_unit_frequency[residual_unit, 1]).astype(jnp.bfloat16)
        )
        mixed = jnp.einsum(
            "cli,io->clo",
            branch,
            lax.all_gather(pointwise_conv_weight[residual_unit], "tm", axis=0, tiled=True),
            preferred_element_type=jnp.float32,
        )
        state = state + mixed
    decoded = state.astype(jnp.bfloat16)
    sample_pos = tm_index * sample_rows + jnp.arange(sample_rows)
    valid = sample_pos[None, :] < stride * lengths[:, None]
    partial_sum = jnp.sum(jnp.where(valid[:, :, None], state * state, jnp.float32(0.0)), axis=1)
    summed = lax.psum_scatter(partial_sum, "tm", scatter_dimension=1, tiled=True)
    count = (stride * lengths[:, None]).astype(jnp.float32)
    energy = jnp.log(summed / count + 1e-06)
    return (decoded, energy)


def solution(mesh):
    in_specs = (
        P("clip", "tm", None),
        P(),
        P(),
        P(),
        P(),
        P("tm", None, "clip"),
        P(None, None, "clip"),
        P(None, None, "tm", "clip"),
        P(None, "tm", "clip"),
    )
    out_specs = (P(None, "tm", "clip"), P(None, ("clip", "tm")))
    return jax.shard_map(body, mesh=mesh, in_specs=in_specs, out_specs=out_specs, check_vma=False)
```

profile of v0, /device:TPU:1, one launch (start us, length us, event | category | flops | bytes accessed | tf_op | source)
XLA Modules:
  0.0 429.4 jit_solution(12332743638398715507)
XLA Ops:
  8.0 1.7 fusion.126
  10.4 10.6 %all_gather.30 = bf16[8,16,64]{2,1,0:T(8,128)(2,1)S(1)} all-gather(bf16[2,16,64]{2,1,0:T(8,128)(2,1)} %param.9), channel_id=1, replica_groups=mesh['clip'=4,'tm'=32] {'clip'}, dimensions={0}, use_global_device_ids=true | all-gather | bytes 20480 | tf_op jit(solution)/shard_map/all_gather | solution.py:66
  23.0 7.0 %collective-permute-start = (bf16[8,3,64]{2,1,0:T(4,128)(2,1)S(1)}, bf16[8,3,64]{2,1,0:T(4,128)(2,1)S(1)}, u32[]{:S(2)}, u32[]{:S(2)}) collective-permute-start(bf16[8,3,64]{2,1,0:T(4,128)(2,1)S(1)} %get-tuple-element.16), channel_id=1, source_target_pairs={{0,1},{1,2},{2,3},{3,4},{4,5},{5,6},{6,7},{7,8},{8,9},{9,10},{10,1... | collective-permute-start | bytes 9224 | tf_op jit(solution)/shard_map/ppermute | solution.py:12
  30.0 1.9 collective-permute-start.1
  33.2 2.2 collective-permute-done.1
  37.2 4.2 add_convert_fusion.3
  41.6 1.9 collective-permute-start.2
  43.5 2.4 collective-permute-start.3
  45.9 40.6 %all-gather.12.cloned.1.call-done = bf16[2048,16,256]{2,1,0:T(8,128)(2,1)} async-done(((bf16[64,16,256]{2,1,0:T(8,128)(2,1)}), bf16[2048,16,256]{2,1,0:T(8,128)(2,1)}) %all-gather.12.cloned.1.call-update) | async-done | bytes 16777232 | tf_op jit(solution)/shard_map/all_gather | solution.py:78
  86.5 24.1 %copy.17 = bf16[2048,16,256]{0,2,1:T(8,128)(2,1)} copy(bf16[2048,16,256]{2,1,0:T(8,128)(2,1)} %all-gather.12.cloned.1.call-done) | data formatting | bytes 33554432 | tf_op jit(solution)/shard_map/reshape | solution.py:81
  110.6 9.2 %fusion = f32[8,18,16,256]{3,1,2,0:T(8,128)S(1)} fusion(bf16[2048,16,256]{0,2,1:T(8,128)(2,1)} %copy.17, bf16[8,1,2048]{2,1,0:T(2,128)(2,1)S(1)} %collective-permute-done.3, bf16[8,16,2048]{2,1,0:T(8,128)(2,1)} %copy-done.1, bf16[8,1,2048]{2,1,0:T(2,128)(2,1)S(1)} %collective-permute-done.2), kind=kOutput, calls=%fused_computation.1 | convolution fusion | flops 2417688576 | bytes 19726336 | tf_op jit(solution)/shard_map/dot_general | solution.py:80
  120.2 3.9 fusion.73
  124.1 2.7 collective-permute-start.4
  126.8 1.9 collective-permute-start.5
  128.8 3.5 collective-permute-done.5
  134.7 35.7 %all-gather.14.cloned.1.call-done = bf16[8,134,1024]{2,1,0:T(8,128)(2,1)} async-done(((bf16[8,134,256]{2,1,0:T(8,128)(2,1)}), bf16[8,134,1024]{2,1,0:T(8,128)(2,1)}) %all-gather.14.cloned.1.call-update) | async-done | bytes 2195472 | tf_op jit(solution)/shard_map/all_gather | solution.py:44
  170.4 2.6 fusion.20
  177.6 5.1 %add_convert_fusion.2 = bf16[8,128,256]{2,1,0:T(8,128)(2,1)} fusion(f32[8,128,256]{2,1,0:T(8,128)S(1)} %fusion.20, f32[8,128,256]{2,1,0:T(8,128)S(1)} %fusion.22, f32[8,128,256]{2,1,0:T(8,128)S(1)} %fusion.24, f32[8,128,256]{2,1,0:T(8,128)S(1)} %fusion.26, f32[8,128,256]{2,1,0:T(8,128)S(1)} %fusion.28, f32[8,128,256]{2,1,0:T(8,128)S(1)} %fusion.30, ...), kind=kOutput, calls=%fused_computation.60 | convolution fusion | flops 539754496 | bytes 9438208 | tf_op jit(solution)/shard_map/cli,io->clo/dot_general | solution.py:33
  183.4 26.4 %all-gather.1 = bf16[1,1024,256]{2,1,0:T(8,128)(2,1)S(1)} all-gather(bf16[1,32,256]{2,1,0:T(8,128)(2,1)S(1)} %get-tuple-element.15), channel_id=3, replica_groups=mesh['clip'=4,'tm'=32] {'tm'}, dimensions={1}, use_global_device_ids=true | all-gather | bytes 540672 | tf_op jit(solution)/shard_map/all_gather | solution.py:108
  209.7 8.6 %all-gather.16.cloned.1.call-done = bf16[8,128,1024]{2,1,0:T(8,128)(2,1)} async-done(((bf16[8,128,256]{2,1,0:T(8,128)(2,1)}), bf16[8,128,1024]{2,1,0:T(8,128)(2,1)}) %all-gather.16.cloned.1.call-update) | async-done | bytes 2097168 | tf_op jit(solution)/shard_map/all_gather | solution.py:44
  218.3 5.9 %add_convert_fusion.1 = (bf16[8,128,256]{2,1,0:T(8,128)(2,1)S(1)}, f32[8,128,256]{2,1,0:T(8,128)S(1)}) fusion(f32[256]{0:T(256)S(1)} %bitcast.150, bf16[8,128,1024]{2,1,0:T(8,128)(2,1)} %all-gather.16.cloned.1.call-done, bf16[1,1024,256]{2,1,0:T(8,128)(2,1)S(1)} %all-gather.1, f32[8,16,8,256]{3,1,2,0:T(8,128)S(1)} %pad_maximum_fusion), kind=kOutput, calls=%fused_computation.59 | convolution fusion | flops 538443776 | bytes 5243904 | tf_op jit(solution)/shard_map/cli,io->clo/dot_general | solution.py:105
  224.3 4.6 %collective-permute-start.6 = (bf16[8,9,256]{2,1,0:T(8,128)(2,1)S(1)}, bf16[8,9,256]{2,1,0:T(8,128)(2,1)S(1)}, u32[]{:S(2)}, u32[]{:S(2)}) collective-permute-start(bf16[8,9,256]{2,1,0:T(8,128)(2,1)S(1)} %get-tuple-element.6), channel_id=1, source_target_pairs={{0,1},{1,2},{2,3},{3,4},{4,5},{5,6},{6,7},{7,8},{8,9},{9,10},{10,1... | collective-permute-start | bytes 110600 | tf_op jit(solution)/shard_map/ppermute | solution.py:12
  228.9 1.9 collective-permute-start.7
  230.8 3.6 collective-permute-done.7
  235.7 33.0 %all-gather.24.cloned.1.call-done = bf16[1,7,1024,256]{3,2,1,0:T(8,128)(2,1)} async-done(((bf16[1,7,32,256]{3,2,1,0:T(8,128)(2,1)}), bf16[1,7,1024,256]{3,2,1,0:T(8,128)(2,1)}) %all-gather.24.cloned.1.call-update) | async-done | bytes 3670032 | tf_op jit(solution)/shard_map/all_gather | solution.py:98
  268.7 37.3 %all-gather.18.cloned.1.call-done = bf16[8,146,1024]{2,1,0:T(8,128)(2,1)} async-done(((bf16[8,146,256]{2,1,0:T(8,128)(2,1)}), bf16[8,146,1024]{2,1,0:T(8,128)(2,1)}) %all-gather.18.cloned.1.call-update) | async-done | bytes 2392080 | tf_op jit(solution)/shard_map/all_gather | solution.py:44
  306.1 2.6 fusion.6
  313.3 5.1 %add_convert_fusion = bf16[8,128,256]{2,1,0:T(8,128)(2,1)} fusion(f32[8,128,256]{2,1,0:T(8,128)S(1)} %fusion.6, f32[8,128,256]{2,1,0:T(8,128)S(1)} %fusion.8, f32[8,128,256]{2,1,0:T(8,128)S(1)} %fusion.10, f32[8,128,256]{2,1,0:T(8,128)S(1)} %fusion.12, f32[8,128,256]{2,1,0:T(8,128)S(1)} %fusion.14, f32[8,128,256]{2,1,0:T(8,128)S(1)} %fusion.16, ...), kind=kOutput, calls=%fused_computation.58 | convolution fusion | flops 539754496 | bytes 9438208 | tf_op jit(solution)/shard_map/cli,io->clo/dot_general | solution.py:33
  319.7 26.4 %all-gather.3 = bf16[1,1024,256]{2,1,0:T(8,128)(2,1)S(1)} all-gather(bf16[1,32,256]{2,1,0:T(8,128)(2,1)S(1)} %get-tuple-element.14), channel_id=5, replica_groups=mesh['clip'=4,'tm'=32] {'tm'}, dimensions={1}, use_global_device_ids=true | all-gather | bytes 540672 | tf_op jit(solution)/shard_map/all_gather | solution.py:108
  346.2 7.9 %all-gather.20.cloned.1.call-done = bf16[8,128,1024]{2,1,0:T(8,128)(2,1)} async-done(((bf16[8,128,256]{2,1,0:T(8,128)(2,1)}), bf16[8,128,1024]{2,1,0:T(8,128)(2,1)}) %all-gather.20.cloned.1.call-update) | async-done | bytes 2097168 | tf_op jit(solution)/shard_map/all_gather | solution.py:44
  354.1 3.1 select_reduce_fusion
  357.2 64.7 %all-reduce = f32[8,256]{1,0:T(8,128)S(1)} all-reduce(f32[8,256]{1,0:T(8,128)S(1)} %get-tuple-element.4), channel_id=6, replica_groups=mesh['clip'=4,'tm'=32] {'tm'}, use_global_device_ids=true, to_apply=%region_1.2.clone | all-reduce | flops 2048 | bytes 16384
  (80 shorter events, 21.9 us)
Async XLA Ops:
  7.2 28.2 %copy-start = (bf16[7,64,2048]{2,1,0:T(8,128)(2,1)S(1)}, bf16[7,64,2048]{2,1,0:T(8,128)(2,1)}, u32[]{:S(2)}) copy-start(bf16[7,64,2048]{2,1,0:T(8,128)(2,1)} %param.12) | copy-start | bytes 5505028
  7.2 79.4 %all-gather.12.cloned.1.call-start = ((), (), s32[]{:S(2)}) async-start(), calls=%async_computation | async-start | bytes 17301504 | tf_op jit(solution)/shard_map/all_gather | solution.py:78
  7.9 126.8 %all-gather.22.cloned.1.call-start = ((), (), s32[]{:S(2)}) async-start(), calls=%async_computation.5 | async-start | bytes 3784704 | tf_op jit(solution)/shard_map/all_gather | solution.py:98
  9.6 160.7 %all-gather.14.cloned.1.call-start = ((), (), s32[]{:S(2)}) async-start(), calls=%async_computation.1 | async-start | bytes 2785280 | tf_op jit(solution)/shard_map/all_gather | solution.py:44
  23.0 12.9 %collective-permute-start = (bf16[8,3,64]{2,1,0:T(4,128)(2,1)S(1)}, bf16[8,3,64]{2,1,0:T(4,128)(2,1)S(1)}, u32[]{:S(2)}, u32[]{:S(2)}) collective-permute-start(bf16[8,3,64]{2,1,0:T(4,128)(2,1)S(1)} %get-tuple-element.16), channel_id=1, source_target_pairs={{0,1},{1,2},{2,3},{3,4},{4,5},{5,6},{6,7},{7,8},{8,9},{9,10},{10,1... | collective-permute-start | bytes 9224 | tf_op jit(solution)/shard_map/ppermute | solution.py:12
  30.0 5.4 %collective-permute-start.1 = (bf16[8,3,64]{2,1,0:T(4,128)(2,1)S(1)}, bf16[8,3,64]{2,1,0:T(4,128)(2,1)S(1)}, u32[]{:S(2)}, u32[]{:S(2)}) collective-permute-start(bf16[8,3,64]{2,1,0:T(4,128)(2,1)S(1)} %get-tuple-element.17), channel_id=1, source_target_pairs={{1,0},{2,1},{3,2},{4,3},{5,4},{6,5},{7,6},{8,7},{9,8},{10,9},{11,1... | collective-permute-start | bytes 9224 | tf_op jit(solution)/shard_map/ppermute | solution.py:15
  36.5 0.7 copy-start.9
  37.2 8.7 %copy-start.3 = (f32[2,2,256]{2,1,0:T(2,128)S(1)}, f32[2,2,256]{2,1,0:T(2,128)}, u32[]{:S(2)}) copy-start(f32[2,2,256]{2,1,0:T(2,128)} %param.15) | copy-start | bytes 12292
  41.4 4.5 %copy-start.1 = (bf16[8,16,2048]{2,1,0:T(8,128)(2,1)}, bf16[8,16,2048]{2,1,0:T(8,128)(2,1)S(1)}, u32[]{:S(2)}) copy-start(bf16[8,16,2048]{2,1,0:T(8,128)(2,1)S(1)} %add_convert_fusion.3) | copy-start | bytes 1572868
  41.6 69.1 %collective-permute-start.2 = (bf16[8,1,2048]{2,1,0:T(2,128)(2,1)S(1)}, bf16[8,1,2048]{2,1,0:T(2,128)(2,1)S(1)}, u32[]{:S(2)}, u32[]{:S(2)}) collective-permute-start(bf16[8,1,2048]{2,1,0:T(2,128)(2,1)S(1)} %get-tuple-element.10), channel_id=1, source_target_pairs={{0,1},{1,2},{2,3},{3,4},{4,5},{5,6},{6,7},{7,8},{8,9},{9,10},{10,1... | collective-permute-start | bytes 98312 | tf_op jit(solution)/shard_map/ppermute | solution.py:12
  43.5 67.1 %collective-permute-start.3 = (bf16[8,1,2048]{2,1,0:T(2,128)(2,1)S(1)}, bf16[8,1,2048]{2,1,0:T(2,128)(2,1)S(1)}, u32[]{:S(2)}, u32[]{:S(2)}) collective-permute-start(bf16[8,1,2048]{2,1,0:T(2,128)(2,1)S(1)} %get-tuple-element.11), channel_id=1, source_target_pairs={{1,0},{2,1},{3,2},{4,3},{5,4},{6,5},{7,6},{8,7},{9,8},{10,9},{11,1... | collective-permute-start | bytes 98312 | tf_op jit(solution)/shard_map/ppermute | solution.py:15
  124.1 4.7 %collective-permute-start.4 = (bf16[8,3,256]{2,1,0:T(4,128)(2,1)S(1)}, bf16[8,3,256]{2,1,0:T(4,128)(2,1)S(1)}, u32[]{:S(2)}, u32[]{:S(2)}) collective-permute-start(bf16[8,3,256]{2,1,0:T(4,128)(2,1)S(1)} %get-tuple-element.8), channel_id=1, source_target_pairs={{0,1},{1,2},{2,3},{3,4},{4,5},{5,6},{6,7},{7,8},{8,9},{9,10},{10,1... | collective-permute-start | bytes 36872 | tf_op jit(solution)/shard_map/ppermute | solution.py:12
  126.8 5.5 %collective-permute-start.5 = (bf16[8,3,256]{2,1,0:T(4,128)(2,1)S(1)}, bf16[8,3,256]{2,1,0:T(4,128)(2,1)S(1)}, u32[]{:S(2)}, u32[]{:S(2)}) collective-permute-start(bf16[8,3,256]{2,1,0:T(4,128)(2,1)S(1)} %get-tuple-element.9), channel_id=1, source_target_pairs={{1,0},{2,1},{3,2},{4,3},{5,4},{6,5},{7,6},{8,7},{9,8},{10,9},{11,1... | collective-permute-start | bytes 36872 | tf_op jit(solution)/shard_map/ppermute | solution.py:15
  133.3 85.1 %all-gather.16.cloned.1.call-start = ((), (), s32[]{:S(2)}) async-start(), calls=%async_computation.2 | async-start | bytes 2621440 | tf_op jit(solution)/shard_map/all_gather | solution.py:44
  170.4 2.9 copy-start.5
  170.4 3.6 copy-start.8
  177.6 5.8 %copy-start.2 = (bf16[2,32,256]{2,1,0:T(8,128)(2,1)S(1)}, bf16[2,32,256]{2,1,0:T(8,128)(2,1)}, u32[]{:S(2)}) copy-start(bf16[2,32,256]{2,1,0:T(8,128)(2,1)} %param.17) | copy-start | bytes 98308
  182.7 86.0 %all-gather.24.cloned.1.call-start = ((), (), s32[]{:S(2)}) async-start(), calls=%async_computation.6 | async-start | bytes 3784704 | tf_op jit(solution)/shard_map/all_gather | solution.py:98
  183.3 122.8 %all-gather.18.cloned.1.call-start = ((), (), s32[]{:S(2)}) async-start(), calls=%async_computation.3 | async-start | bytes 3112960 | tf_op jit(solution)/shard_map/all_gather | solution.py:44
  224.3 6.5 %collective-permute-start.6 = (bf16[8,9,256]{2,1,0:T(8,128)(2,1)S(1)}, bf16[8,9,256]{2,1,0:T(8,128)(2,1)S(1)}, u32[]{:S(2)}, u32[]{:S(2)}) collective-permute-start(bf16[8,9,256]{2,1,0:T(8,128)(2,1)S(1)} %get-tuple-element.6), channel_id=1, source_target_pairs={{0,1},{1,2},{2,3},{3,4},{4,5},{5,6},{6,7},{7,8},{8,9},{9,10},{10,1... | collective-permute-start | bytes 110600 | tf_op jit(solution)/shard_map/ppermute | solution.py:12
  228.9 5.6 %collective-permute-start.7 = (bf16[8,9,256]{2,1,0:T(8,128)(2,1)S(1)}, bf16[8,9,256]{2,1,0:T(8,128)(2,1)S(1)}, u32[]{:S(2)}, u32[]{:S(2)}) collective-permute-start(bf16[8,9,256]{2,1,0:T(8,128)(2,1)S(1)} %get-tuple-element.7), channel_id=1, source_target_pairs={{1,0},{2,1},{3,2},{4,3},{5,4},{6,5},{7,6},{8,7},{9,8},{10,9},{11,1... | collective-permute-start | bytes 110600 | tf_op jit(solution)/shard_map/ppermute | solution.py:15
  235.5 118.6 %all-gather.20.cloned.1.call-start = ((), (), s32[]{:S(2)}) async-start(), calls=%async_computation.4 | async-start | bytes 2621440 | tf_op jit(solution)/shard_map/all_gather | solution.py:44
  306.0 2.9 copy-start.6
  306.0 3.6 copy-start.7
  313.3 5.1 %copy-start.10 = (u32[128]{0:T(128)S(1)}, u32[128]{0:T(128)}, u32[]{:S(2)}) copy-start(u32[128]{0:T(128)} %constant.34) | copy-start | bytes 1540
  313.3 32.7 %copy-start.4 = (s32[8]{0:T(128)S(1)}, s32[8]{0:T(128)}, u32[]{:S(2)}) copy-start(s32[8]{0:T(128)} %param.11) | copy-start | bytes 100
Sparse Core Ops, SparseCore 0:
  10.3 76.2 all-gather.11
  88.9 45.7 all-gather.21
  136.4 33.9 all-gather.13
  182.8 35.4 all-gather.15
  220.5 48.1 all-gather.23
  270.3 35.7 all-gather.17
  318.6 35.4 all-gather.19
where the time goes:
time: 433 us; the launch traced here: 429 us
  waiting for transfers between devices  175 us (40%)
  blocking collectives  128 us (30%)
  matrix products  47.5 us (11%)
  local copies, waits for them, and re-layouts  29.5 us (7%)
  starting transfers between devices  25.1 us (6%)
  between operations  15.2 us (4%)
  other arithmetic  9.07 us (2%)
    all_gather x4, waiting for transfers between devices, widen(): return lax.all_gather(value, 'clip', axis=2, tiled=True)  89.5 us
    unnamed x1, blocking collectives  64.7 us
    all_gather x2, blocking collectives, body(): lax.all_gather(pointwise_conv_weight[residual_unit], 'tm', axis=0, tiled=...  52.7 us
    all_gather x1, waiting for transfers between devices, body(): add_piece = lax.all_gather(upsample_weight, 'tm', axis=0, tiled=True)  40.6 us
    all_gather x2, waiting for transfers between devices, body(): lax.all_gather(dilated_conv_weight[residual_unit], 'tm', axis=1, tiled=True)  34.2 us
    dot_general x21, matrix products, kernel_tap_count(): jnp.einsum('cli,io->clo', replay_window, weight_bundle[kernel_tap], prefe...  29.3 us
    reshape x1, local copies, waits for them, and re-layouts, body(): add_piece.reshape(rows, upk * c1_local)  24.1 us
    ppermute x4, starting transfers between devices, padded(): lax.ppermute(lax.slice_in_dim(block, block.shape[dim] - width, None, axis...  16.2 us
  transfers between devices with their start and end apart: 15, of which 10 were waited for; matrix products, arithmetic and copies ran while one was open for 13% of the time, Pallas kernels for 0%

commit v1 on v0

v1 whole, which is shorter than its diff:
```python
import functools
import math

import jax
import jax.numpy as jnp
from jax import lax
from jax.experimental import pallas as pl
from jax.experimental.pallas import tpu as pltpu
from jax.sharding import Mesh
from jax.sharding import PartitionSpec as P

BF = jnp.bfloat16
F32 = jnp.float32
SIN2 = (
    9.869603157043457,
    -32.469581604003906,
    42.72538375854492,
    -30.085952758789062,
    12.990730285644531,
    -3.2729458808898926,
)
ROW_CHUNK = 256
EDGE = 2
VMEM = 56 * 1024 * 1024


def snake(value, turns, inverse):
    u = value * turns
    r = u - jnp.round(u)
    z = r * r
    p = jnp.full_like(z, SIN2[-1])
    for coefficient in SIN2[-2::-1]:
        p = p * z + coefficient
    return value + (p * z) * inverse


def entry_kernel(lat_ref, w_ref, freq_ref, s0_ref):
    width = 256
    for n in range(s0_ref.shape[1] // width):
        cols = pl.ds(n * width, width)
        pre = jnp.dot(lat_ref[...], w_ref[:, cols], preferred_element_type=F32)
        s0_ref[:, cols] = snake(pre, freq_ref[0:1, cols], freq_ref[1:2, cols]).astype(BF)


def upsample_kernel(slots, flag_ref, s0_ref, own_ref, other_ref, out_ref, w_s, prod_s, x_s):
    step, steps = pl.program_id(0), pl.num_programs(0)
    groups, rows, cols = own_ref.shape
    half = cols // 2

    @pl.when(step == 0)
    def _():
        @pl.when(flag_ref[0] == 0)
        def _():
            for g in range(groups):
                w_s[pl.ds(2 * g * rows, rows), :] = own_ref[g]
                w_s[pl.ds((2 * g + 1) * rows, rows), :] = other_ref[g]

        @pl.when(flag_ref[0] != 0)
        def _():
            for g in range(groups):
                w_s[pl.ds(2 * g * rows, rows), :] = other_ref[g]
                w_s[pl.ds((2 * g + 1) * rows, rows), :] = own_ref[g]

        prod_s[0:8, :] = jnp.zeros((8, cols), F32)
        prod_s[prod_s.shape[0] - 8 :, :] = jnp.zeros((8, cols), F32)

    chunk = s0_ref.shape[0]
    at = pl.multiple_of(8 + step * chunk, 8)
    prod_s[pl.ds(at, chunk), :] = jnp.dot(s0_ref[...], w_s[...], preferred_element_type=F32)

    @pl.when(step == steps - 1)
    def _():
        total = prod_s.shape[0] - 16
        pad = EDGE * slots
        x_s[0:pad, :] = jnp.zeros((pad, half), F32)
        x_s[x_s.shape[0] - pad :, :] = jnp.zeros((pad, half), F32)
        low = flag_ref[1] == 0
        for r in range(0, total, chunk):
            centre = prod_s[8 + r : 8 + r + chunk, :half]
            before = prod_s[8 - slots + r : 8 - slots + r + chunk, half:]
            after = prod_s[8 + slots + r : 8 + slots + r + chunk, half:]
            x_s[pad + r : pad + r + chunk, :] = centre + jnp.where(low, before, after)
        window = out_ref.shape[1]
        own = window - 2 * pad
        for d in range(out_ref.shape[0]):
            out_ref[d] = x_s[d * own : d * own + window, :].astype(BF)


def taps_to_shift(phases, dilation, tap, phase):
    moved = phase + dilation * (tap - 3)
    return moved % phases, moved // phases


def fill(act_s, lhs_s, dilation, slots, first, rows):
    taps, phases = lhs_s.shape[0], act_s.shape[0]
    wanted = {}
    for t in range(taps):
        for s in range(phases):
            wanted.setdefault(taps_to_shift(phases, dilation, t, s), []).append((t, s))
    for (source, shift), uses in sorted(wanted.items()):
        at = 8 + first + shift * slots
        piece = act_s[source, at : at + rows, :].astype(BF)
        for t, s in uses:
            lhs_s[t, s * rows : (s + 1) * rows, :] = piece


def conv(lhs_s, w_ref, acc_s):
    taps = lhs_s.shape[0]
    depth = lhs_s.shape[2]

    def one(t):
        w = w_ref[0, :, t].reshape(depth, w_ref.shape[-1])
        return jnp.dot(lhs_s[t], w, preferred_element_type=F32)

    acc_s[...] = one(0)

    @pl.loop(1, taps)
    def _(t):
        acc_s[...] += one(t)


def unit0_kernel(slots, x_ref, w_ref, pw_ref, freq_ref, out_ref, act_s, lhs_s, acc_s, b_s):
    y = pl.program_id(0)
    groups, phases, halves, rows, lanes = x_ref.shape

    @pl.when(y == 0)
    def _():
        for s in range(phases):
            act_s[s, 0:8, :] = jnp.zeros((8, act_s.shape[2]), F32)
            act_s[s, 8 + rows :, :] = jnp.zeros((8, act_s.shape[2]), F32)
            for g in range(groups):
                for h in range(halves):
                    cols = slice((g * halves + h) * lanes, (g * halves + h + 1) * lanes)
                    v = x_ref[g, s, h].astype(F32)
                    act_s[s, 8 : 8 + rows, cols] = snake(v, freq_ref[0:1, cols], freq_ref[1:2, cols])
        fill(act_s, lhs_s, 1, slots, 0, rows)

    conv(lhs_s, w_ref, acc_s)
    width = acc_s.shape[1]
    cols = pl.ds(pl.multiple_of(y * width, width), width)
    b_s[:, cols] = snake(acc_s[...], freq_ref[2:3, cols], freq_ref[3:4, cols]).astype(BF)

    @pl.when(y == groups - 1)
    def _():
        for g in range(groups):
            w = pw_ref[g].reshape(b_s.shape[1], width)
            acc_s[...] = jnp.dot(b_s[...], w, preferred_element_type=F32)
            for s in range(phases):
                for h in range(halves):
                    at = slice(s * rows, (s + 1) * rows)
                    out_ref[g, at, h * lanes : (h + 1) * lanes] = (
                        acc_s[at, h * lanes : (h + 1) * lanes] + x_ref[g, s, h].astype(F32)
                    )


def unit1_kernel(
    slots, x_ref, w_ref, pw_ref, freq_ref, inside_ref, live_ref, dec_ref, energy_ref, act_s, lhs_s, acc_s, b_s, t_s, o_s
):
    y = pl.program_id(0)
    groups, all_rows, width = x_ref.shape
    phases = act_s.shape[0]
    rows = all_rows // phases
    first = EDGE * slots
    kept = rows - 2 * first
    frames = kept // slots

    @pl.when(y == 0)
    def _():
        for s in range(phases):
            act_s[s, 0:8, :] = jnp.zeros((8, act_s.shape[2]), F32)
            act_s[s, 8 + rows :, :] = jnp.zeros((8, act_s.shape[2]), F32)
            for g in range(groups):
                cols = slice(g * width, (g + 1) * width)
                v = x_ref[g, s * rows : (s + 1) * rows, :]
                act_s[s, 8 : 8 + rows, cols] = (
                    snake(v, freq_ref[0:1, cols], freq_ref[1:2, cols]) * inside_ref[...]
                )
        fill(act_s, lhs_s, 3, slots, first, kept)

    conv(lhs_s, w_ref, acc_s)
    cols = pl.ds(pl.multiple_of(y * width, width), width)
    b_s[:, cols] = snake(acc_s[...], freq_ref[2:3, cols], freq_ref[3:4, cols]).astype(BF)

    @pl.when(y == groups - 1)
    def _():
        for g in range(groups):
            w = pw_ref[g].reshape(b_s.shape[1], width)
            acc_s[...] = jnp.dot(b_s[...], w, preferred_element_type=F32)
            for s in range(phases):
                at = s * rows + first
                acc_s[s * kept : (s + 1) * kept, :] += x_ref[g, at : at + kept, :]
            live = live_ref[...]
            squares = jnp.zeros((kept, width), F32)
            for s in range(phases):
                v = acc_s[s * kept : (s + 1) * kept, :]
                squares += v * v * live
            energy_ref[:, g * width : (g + 1) * width] = squares
            for h in range(width // 128):
                lanes = slice(h * 128, (h + 1) * 128)
                for s in range(phases):
                    t_s[...] = acc_s[s * kept : (s + 1) * kept, lanes]
                    for k in range(slots):
                        o_s[pl.ds(k * frames * phases + s, frames, stride=phases), :] = t_s[
                            pl.ds(k, frames, stride=slots), :
                        ]
                for k in range(slots):
                    dec_ref[g, k, :, lanes] = o_s[k * frames * phases : (k + 1) * frames * phases, :].astype(BF)


def cost(flops, moved):
    return pl.CostEstimate(flops=flops, bytes_accessed=moved, transcendentals=0)


def run_entry(lat, w, freq):
    rows, depth = lat.shape
    c0 = w.shape[1]
    return pl.pallas_call(
        entry_kernel,
        grid=(rows // ROW_CHUNK,),
        in_specs=[
            pl.BlockSpec((ROW_CHUNK, depth), lambda i: (i, 0)),
            pl.BlockSpec((depth, c0), lambda i: (0, 0)),
            pl.BlockSpec((2, c0), lambda i: (0, 0)),
        ],
        out_specs=pl.BlockSpec((ROW_CHUNK, c0), lambda i: (i, 0)),
        out_shape=jax.ShapeDtypeStruct((rows, c0), BF),
        compiler_params=pltpu.CompilerParams(vmem_limit_bytes=VMEM),
        cost_estimate=cost(2 * rows * depth * c0, 2 * rows * c0),
        name="entry",
    )(lat, w, freq)


def run_upsample(flags, s0, own, other, slots, chips):
    rows, c0 = s0.shape
    cols = own.shape[2]
    half = cols // 2
    pad = EDGE * slots
    window = rows // chips + 2 * pad
    whole = pl.BlockSpec(own.shape, lambda i: (0, 0, 0))
    return pl.pallas_call(
        functools.partial(upsample_kernel, slots),
        grid=(rows // ROW_CHUNK,),
        in_specs=[
            pl.BlockSpec(memory_space=pltpu.SMEM),
            pl.BlockSpec((ROW_CHUNK, c0), lambda i: (i, 0)),
            whole,
            whole,
        ],
        out_specs=pl.BlockSpec((chips, window, half), lambda i: (0, 0, 0)),
        out_shape=jax.ShapeDtypeStruct((chips, window, half), BF),
        scratch_shapes=[
            pltpu.VMEM((c0, cols), BF),
            pltpu.VMEM((rows + 16, cols), F32),
            pltpu.VMEM((rows + 2 * pad, half), F32),
        ],
        compiler_params=pltpu.CompilerParams(vmem_limit_bytes=VMEM),
        cost_estimate=cost(2 * rows * c0 * cols, 2 * rows * c0),
        name="upsample",
    )(flags, s0, own, other)


def weight_specs(weights, unit):
    groups, shards, _, kinds, rows, width = weights.shape
    return [
        pl.BlockSpec((1, shards, None, kinds, rows, width), lambda i: (i, 0, unit, 0, 0, 0)),
        pl.BlockSpec((groups, shards, None, None, rows, width), lambda i: (0, 0, unit, kinds - 1, 0, 0)),
    ]


def run_unit0(x, weights, freq, slots):
    groups, phases, halves, rows, lanes = x.shape
    taps = weights.shape[3] - 1
    channels, width = groups * halves * lanes, halves * lanes
    m = phases * rows
    return pl.pallas_call(
        functools.partial(unit0_kernel, slots),
        grid=(groups,),
        in_specs=[
            pl.BlockSpec(x.shape, lambda i: (0, 0, 0, 0, 0)),
            *weight_specs(weights, 0),
            pl.BlockSpec(freq.shape, lambda i: (0, 0)),
        ],
        out_specs=pl.BlockSpec((groups, m, width), lambda i: (0, 0, 0)),
        out_shape=jax.ShapeDtypeStruct((groups, m, width), F32),
        scratch_shapes=[
            pltpu.VMEM((phases, rows + 16, channels), F32),
            pltpu.VMEM((taps, m, channels), BF),
            pltpu.VMEM((m, width), F32),
            pltpu.VMEM((m, channels), BF),
        ],
        compiler_params=pltpu.CompilerParams(vmem_limit_bytes=VMEM),
        cost_estimate=cost(2 * m * (taps + 1) * channels * channels, weights.size),
        name="unit0",
    )(x, weights, weights, freq)


def run_unit1(x, weights, freq, inside, live, slots, phases):
    groups, all_rows, width = x.shape
    rows = all_rows // phases
    kept = rows - 2 * EDGE * slots
    taps = weights.shape[3] - 1
    channels = groups * width
    m = phases * kept
    samples = m // slots
    return pl.pallas_call(
        functools.partial(unit1_kernel, slots),
        grid=(groups,),
        in_specs=[
            pl.BlockSpec(x.shape, lambda i: (0, 0, 0)),
            *weight_specs(weights, 1),
            pl.BlockSpec(freq.shape, lambda i: (0, 0)),
            pl.BlockSpec(inside.shape, lambda i: (0, 0)),
            pl.BlockSpec(live.shape, lambda i: (0, 0)),
        ],
        out_specs=[
            pl.BlockSpec((groups, slots, samples, width), lambda i: (0, 0, 0, 0)),
            pl.BlockSpec((kept, channels), lambda i: (0, 0)),
        ],
        out_shape=[
            jax.ShapeDtypeStruct((groups, slots, samples, width), BF),
            jax.ShapeDtypeStruct((kept, channels), F32),
        ],
        scratch_shapes=[
            pltpu.VMEM((phases, rows + 16, channels), F32),
            pltpu.VMEM((taps, m, channels), BF),
            pltpu.VMEM((m, width), F32),
            pltpu.VMEM((m, channels), BF),
            pltpu.VMEM((kept, 128), F32),
            pltpu.VMEM((m, 128), F32),
        ],
        compiler_params=pltpu.CompilerParams(vmem_limit_bytes=VMEM),
        cost_estimate=cost(2 * m * (taps + 1) * channels * channels, weights.size),
        name="unit1",
    )(x, weights, weights, freq, inside, live)


def freq_rows(alpha):
    return jnp.stack([alpha / math.pi, 1.0 / alpha], axis=-2)


def body(
    latent,
    dest,
    lengths,
    input_conv_weight,
    snake_entry_frequency,
    upsample_weight,
    snake_unit_frequency,
    dilated_conv_weight,
    pointwise_conv_weight,
):
    everyone = ("y", "x", "z", "c")
    blocks = ("x", "z", "y")
    ny, nx, nz, nc = (lax.axis_size(a) for a in everyone)
    iy, ix, iz, ic = (lax.axis_index(a) for a in everyone)
    chips = ny * nx * nz
    here_clips, here_frames, width_in = latent.shape
    clips = dest.shape[0]
    frames = here_frames * nx * nz * nc
    slots = clips // nc
    own_frames = frames // chips
    units, taps = dilated_conv_weight.shape[:2]
    upk, c1_local = upsample_weight.shape[1:]
    phases = upk // 2
    halves = nx * nz // phases
    lanes = c1_local // halves
    first_slot = ic * slots

    weights = jnp.concatenate([dilated_conv_weight, pointwise_conv_weight[:, None]], axis=1)
    shape = weights.shape
    weights = lax.all_gather(weights.reshape(-1, *shape[2:]), everyone, axis=0, tiled=True)
    weights = weights.reshape(ny, nx * nz * nc, *shape)

    packed = latent.transpose(1, 0, 2).reshape(here_frames, here_clips * width_in)
    packed = jnp.broadcast_to(packed[None], (ny * nx * nz * nc,) + packed.shape)
    packed = lax.all_to_all(packed, everyone, 0, 0, tiled=True)
    order = []
    for s in range(phases):
        near = s + phases // 2
        far = s + 3 * phases // 2 if s < phases // 2 else s - phases // 2
        order += [near, far]
    up = upsample_weight.transpose(1, 0, 2)
    up = jnp.stack([up[q] for q in order]).reshape(phases, 2, -1, halves, lanes)
    up = up.transpose(0, 3, 2, 1, 4).reshape(phases * halves, -1, 2 * lanes)
    up, packed = lax.optimization_barrier((up, packed))
    packed = packed.reshape(ny, frames, here_clips, width_in).transpose(0, 2, 1, 3)
    packed = packed.reshape(clips, frames, width_in)
    my_dest = lax.dynamic_slice_in_dim(dest, first_slot, slots)
    my_lengths = lax.dynamic_slice_in_dim(lengths, first_slot, slots)
    picked = jnp.take(packed, my_dest, axis=0)
    live = jnp.arange(frames)[None, :] < my_lengths[:, None]
    picked = jnp.where(live[:, :, None], picked, jnp.zeros_like(picked)).transpose(1, 0, 2)
    reach = input_conv_weight.shape[0] // 2
    picked = jnp.pad(picked, ((reach, reach), (0, 0), (0, 0)))
    picked = jnp.concatenate([picked[t : t + frames] for t in range(2 * reach + 1)], axis=2)
    picked = picked.reshape(frames * slots, -1)
    own = lax.all_to_all(up, ("x", "z"), 0, 0, tiled=True)
    other = lax.ppermute(own, "c", [(i, nc - 1 - i) for i in range(nc)])

    w_in = input_conv_weight.reshape(-1, input_conv_weight.shape[2])
    s0 = run_entry(picked, w_in, freq_rows(snake_entry_frequency))
    flags = jnp.stack([ic, (ix * nz + iz) // (phases // 2 * halves)]).astype(jnp.int32)
    x = run_upsample(flags, s0, own, other, slots, chips)
    x = lax.all_to_all(x, blocks, 0, 0, tiled=True)
    window = x.shape[1]
    x = x.reshape(phases, halves, ny, window, lanes).transpose(2, 0, 1, 3, 4)

    freq = freq_rows(snake_unit_frequency).reshape(1, -1, c1_local)
    freq = lax.all_to_all(jnp.broadcast_to(freq, (ny,) + freq.shape[1:]), "y", 0, 0, tiled=True)
    freq = freq.transpose(1, 0, 2).reshape(units, -1, ny * c1_local)

    x = run_unit0(x, weights, freq[0], slots)

    block = (ix * nz + iz) * ny + iy
    at = block * own_frames - EDGE + jnp.arange(own_frames + 2 * EDGE)
    inside = ((at >= 0) & (at < frames)).astype(F32)
    inside = jnp.broadcast_to(jnp.repeat(inside, slots)[:, None], (window, c1_local))
    at = at[EDGE:-EDGE]
    live = (at[:, None] < my_lengths[None, :]).astype(F32).reshape(-1)
    live = jnp.broadcast_to(live[:, None], (own_frames * slots, c1_local))
    decoded, squares = run_unit1(x, weights, freq[1], inside, live, slots, phases)

    decoded = lax.all_to_all(decoded, "y", 0, 0, tiled=True)
    part = ny // nc
    kept = lax.dynamic_slice_in_dim(decoded, ic * part, part)
    sent = lax.dynamic_slice_in_dim(decoded, (nc - 1 - ic) * part, part)
    came = lax.ppermute(sent, "c", [(i, nc - 1 - i) for i in range(nc)])
    low = ic == 0
    decoded = jnp.stack([jnp.where(low, kept, came), jnp.where(low, came, kept)])
    samples = part * decoded.shape[3]
    decoded = decoded.transpose(0, 2, 1, 3, 4).reshape(clips, samples, c1_local)

    squares = squares.reshape(own_frames, slots, -1).sum(axis=0)
    squares = squares.reshape(slots, ny * nx * nz * nc, -1).transpose(1, 0, 2)
    squares = lax.all_to_all(squares, everyone, 0, 0, tiled=True)
    squares = squares.reshape(chips, clips, -1).sum(axis=0)
    count = (phases * lengths[:, None]).astype(F32)
    energy = jnp.log(squares / count + 1e-06)
    return decoded, energy


def solution(mesh):
    ny = mesh.shape["clip"]
    side = 4
    fine = Mesh(mesh.devices.reshape(ny, side, side, 2), ("y", "x", "z", "c"))
    tm = ("x", "z", "c")
    in_specs = (
        P("y", tm, None),
        P(),
        P(),
        P(),
        P(),
        P(tm, None, "y"),
        P(None, None, "y"),
        P(None, None, tm, "y"),
        P(None, tm, "y"),
    )
    out_specs = (P(None, tm, "y"), P(None, ("y",) + tm))
    return jax.shard_map(body, mesh=fine, in_specs=in_specs, out_specs=out_specs, check_vma=False)
```

time: 433 us -> 207 us (0.48)
  blocking collectives: 128 us -> 0 us
  waiting for transfers between devices: 175 us -> 61.4 us
  Pallas kernels: 0 us -> 58.3 us
  matrix products: 47.5 us -> 0 us
  starting transfers between devices: 25.1 us -> 41 us
    all_gather x7 -> x1, waiting for transfers between devices: 164 us -> 10.8 us  [body(): lax.all_gather(weights.reshape(-1, *shape[2:]), everyone, axis=0, tiled=T...]
    unnamed x1 -> x0, blocking collectives: 64.7 us -> none
    all_gather x3 -> x0, blocking collectives: 63.3 us -> none  [the longest x2 52.7 us: body(): lax.all_gather(pointwise_conv_weight[residual_unit], 'tm', axis=0, tiled=...]
    pallas_call x0 -> x4, Pallas kernels: none -> 58.3 us  [the longest x1 18 us: run_unit0(): pl.pallas_call(functools.partial(unit0_kernel, slots), grid=(groups,), in...]
    all_to_all x0 -> x6, waiting for transfers between devices: none -> 50.7 us  [the longest x1 21.3 us: body(): x = lax.all_to_all(x, blocks, 0, 0, tiled=True)]
    dot_general x24 -> x0, matrix products: 47.5 us -> none  [the longest x21 29.3 us: kernel_tap_count(): jnp.einsum('cli,io->clo', replay_window, weight_bundle[kernel_tap], prefe...]
    all_to_all x0 -> x6, starting transfers between devices: none -> 36.7 us  [the longest x1 11.5 us: body(): packed = lax.all_to_all(packed, everyone, 0, 0, tiled=True)]
    ppermute x8 -> x2, starting transfers between devices: 24.4 us -> 4.21 us  [the longest x1 3.06 us: body(): other = lax.ppermute(own, 'c', [(i, nc - 1 - i) for i in range(nc)])]
  transfers between devices with their start and end apart: 15 -> 9, of which waited for: 10 -> 6; matrix products, arithmetic and copies ran while one was open for 13% -> 13% of each run, Pallas kernels for 0% -> 12%
where the time goes in v1:
time: 207 us; the launch traced here: 206 us
  waiting for transfers between devices  61.4 us (30%)
  Pallas kernels  58.3 us (28%)
  starting transfers between devices  41 us (20%)
  local copies, waits for them, and re-layouts  26.2 us (13%)
  between operations  14.3 us (7%)
  other arithmetic  4.98 us (2%)
    all_to_all x1, waiting for transfers between devices, body(): x = lax.all_to_all(x, blocks, 0, 0, tiled=True)  21.3 us
    pallas_call x1, Pallas kernels, run_unit0(): pl.pallas_call(functools.partial(unit0_kernel, slots), grid=(groups,), in...  18 us
    pallas_call x1, Pallas kernels, run_unit1(): pl.pallas_call(functools.partial(unit1_kernel, slots), grid=(groups,), in...  15.8 us
    pallas_call x1, Pallas kernels, run_entry(): pl.pallas_call(entry_kernel, grid=(rows // ROW_CHUNK,), in_specs=[pl.Bloc...  15.5 us
    all_to_all x1, starting transfers between devices, body(): packed = lax.all_to_all(packed, everyone, 0, 0, tiled=True)  11.5 us
    all_gather x1, waiting for transfers between devices, body(): lax.all_gather(weights.reshape(-1, *shape[2:]), everyone, axis=0, tiled=T...  10.8 us
    all_to_all x1, waiting for transfers between devices, body(): squares = lax.all_to_all(squares, everyone, 0, 0, tiled=True)  9.7 us
    pallas_call x1, Pallas kernels, run_upsample(): pl.pallas_call(functools.partial(upsample_kernel, slots), grid=(rows // R...  9.02 us
  transfers between devices with their start and end apart: 9, of which 6 were waited for; matrix products, arithmetic and copies ran while one was open for 13% of the time, Pallas kernels for 12%

profile of v1, /device:TPU:1, one launch (start us, length us, event | category | flops | bytes accessed | tf_op | source)
XLA Modules:
  0.0 206.2 jit_solution(10237769384763288589)
XLA Ops:
  7.2 1.7 pad_maximum_fusion
  9.8 0.9 broadcast_in_dim.64
  10.6 11.5 %all-to-all-start = ((bf16[128,16,128]{2,1,0:T(8,128)(2,1)}), bf16[128,16,128]{2,1,0:T(8,128)(2,1)S(1)}, u32[]{:S(2)}, u32[]{:S(2)}) async-start(bf16[128,16,128]{2,1,0:T(8,128)(2,1)} %broadcast_in_dim.64), calls=%async_computation | async-start | bytes 1048576 | tf_op jit(solution)/shard_map/all_to_all | solution.py:376
  22.2 1.1 fusion.6
  23.3 1.6 stack.42
  25.5 1.1 reshape.101
  28.2 8.6 %all-to-all-done = bf16[128,16,128]{2,1,0:T(8,128)(2,1)S(1)} async-done(((bf16[128,16,128]{2,1,0:T(8,128)(2,1)}), bf16[128,16,128]{2,1,0:T(8,128)(2,1)S(1)}, u32[]{:S(2)}, u32[]{:S(2)}) %all-to-all-start) | async-done | bytes 524320 | tf_op jit(solution)/shard_map/all_to_all | solution.py:376
  37.9 3.6 %all-to-all-start.1 = ((bf16[16,64,256]{2,1,0:T(8,128)(2,1)}), bf16[16,64,256]{2,1,0:T(8,128)(2,1)S(1)}, u32[]{:S(2)}, u32[]{:S(2)}) async-start(bf16[16,64,256]{2,1,0:T(8,128)(2,1)} %reshape.101), calls=%async_computation.1 | async-start | bytes 1048576 | tf_op jit(solution)/shard_map/all_to_all | solution.py:397
  42.2 0.8 fusion
  43.0 0.8 fusion.1
  43.9 0.9 fusion.2
  45.6 0.8 fusion.3
  46.4 4.1 %all-to-all-done.1.own_ref = bf16[16,64,256]{2,1,0:T(8,128)(2,1)S(1)} async-done(((bf16[16,64,256]{2,1,0:T(8,128)(2,1)}), bf16[16,64,256]{2,1,0:T(8,128)(2,1)S(1)}, u32[]{:S(2)}, u32[]{:S(2)}) %all-to-all-start.1) | async-done | bytes 524320 | tf_op jit(solution)/shard_map/all_to_all | solution.py:397
  51.1 3.8 %all-to-all-start.3 = ((f32[4,8,256]{2,1,0:T(8,128)}), f32[4,8,256]{2,1,0:T(8,128)S(1)}, u32[]{:S(2)}, u32[]{:S(2)}) async-start(f32[4,8,256]{2,1,0:T(8,128)} %broadcast_in_dim.70), calls=%async_computation.3 | async-start | bytes 65536 | tf_op jit(solution)/shard_map/all_to_all | solution.py:409
  54.9 3.1 %collective-permute-start = (bf16[16,64,256]{2,1,0:T(8,128)(2,1)S(1)}, bf16[16,64,256]{2,1,0:T(8,128)(2,1)S(1)}, u32[]{:S(2)}, u32[]{:S(2)}) collective-permute-start(bf16[16,64,256]{2,1,0:T(8,128)(2,1)S(1)} %all-to-all-done.1.own_ref), channel_id=1, source_target_pairs={{0,1},{1,0},{2,3},{3,2},{4,5},{5,4},{6,7},{7,6},{8,9},{9,8},{10,11... | collective-permute-start | bytes 1572872 | tf_op jit(solution)/shard_map/ppermute | solution.py:398
  59.6 3.3 %copy.25 = bf16[512,4,448]{2,1,0:T(4,128)(2,1)S(1)} copy(bf16[512,4,448]{0,2,1:T(8,128)(2,1)} %fusion.5) | data formatting | bytes 3670016 | tf_op jit(solution)/shard_map/concatenate | solution.py:395
  63.0 2.4 %reshape.104.lat_ref = bf16[2048,448]{1,0:T(8,128)(2,1)} reshape(bf16[512,4,448]{2,1,0:T(4,128)(2,1)S(1)} %copy.25) | data formatting | bytes 3670016 | tf_op jit(solution)/shard_map/reshape | solution.py:396
  65.4 15.5 %entry.1.s0_ref = bf16[2048,2048]{1,0:T(8,128)(2,1)} custom-call(bf16[2048,448]{1,0:T(8,128)(2,1)} %reshape.104.lat_ref, bf16[448,2048]{1,0:T(8,128)(2,1)} %bitcast.66, f32[2,2048]{1,0:T(2,128)} %pad_maximum_fusion.1.freq_ref), custom_call_target="tpu_custom_call" | custom-call | flops 3758096384 | bytes 8388608 | tf_op jit(solution)/shard_map/entry/pallas_call | solution.py:217
  81.7 9.0 %upsample.1 = bf16[64,48,128]{2,1,0:T(8,128)(2,1)} custom-call(s32[2]{0:T(128)} %pad_add_fusion.flag_ref, bf16[2048,2048]{1,0:T(8,128)(2,1)} %entry.1.s0_ref, bf16[16,64,256]{2,1,0:T(8,128)(2,1)} %copy-done, bf16[16,64,256]{2,1,0:T(8,128)(2,1)} %copy-done.2), custom_call_target="tpu_custom_call" | custom-call | flops 2147483648 | bytes 8388608 | tf_op jit(solution)/shard_map/upsample/pallas_call | solution.py:240
  90.8 7.3 %all-to-all-start.2 = ((bf16[64,48,128]{2,1,0:T(8,128)(2,1)}), bf16[64,48,128]{2,1,0:T(8,128)(2,1)S(1)}, u32[]{:S(2)}, u32[]{:S(2)}) async-start(bf16[64,48,128]{2,1,0:T(8,128)(2,1)} %upsample.1), calls=%async_computation.2 | async-start | bytes 1572864 | tf_op jit(solution)/shard_map/all_to_all | solution.py:404
  99.1 21.3 %all-to-all-done.2 = bf16[64,48,128]{2,1,0:T(8,128)(2,1)S(1)} async-done(((bf16[64,48,128]{2,1,0:T(8,128)(2,1)}), bf16[64,48,128]{2,1,0:T(8,128)(2,1)S(1)}, u32[]{:S(2)}, u32[]{:S(2)}) %all-to-all-start.2) | async-done | bytes 786464 | tf_op jit(solution)/shard_map/all_to_all | solution.py:404
  120.4 1.0 copy.33
  121.4 10.8 %all-gather.2.cloned.1.call-done = bf16[2048,32,256]{2,1,0:T(8,128)(2,1)} async-done(((bf16[16,32,256]{2,1,0:T(8,128)(2,1)}), bf16[2048,32,256]{2,1,0:T(8,128)(2,1)}) %all-gather.2.cloned.1.call-update) | async-done | bytes 33554448 | tf_op jit(solution)/shard_map/all_gather | solution.py:371
  132.1 18.0 %unit0.1.x_ref = f32[4,384,256]{2,1,0:T(8,128)} custom-call(bf16[4,8,2,48,128]{4,3,2,1,0:T(8,128)(2,1)} %bitcast.50, bf16[4,32,2,8,32,256]{5,4,3,2,1,0:T(8,128)(2,1)} %bitcast.45, bf16[4,32,2,8,32,256]{5,4,3,2,1,0:T(8,128)(2,1)} %bitcast.46, f32[4,1024]{1,0:T(4,128)} %bitcast.61), custom_call_target="tpu_custom_call" | custom-call | flops 6442450944 | bytes 16777216 | tf_op jit(solution)/shard_map/unit0/pallas_call | solution.py:275
  151.4 15.8 %unit1.1 = (bf16[4,4,64,256]{3,2,1,0:T(8,128)(2,1)}, f32[32,1024]{1,0:T(8,128)}) custom-call(f32[4,384,256]{2,1,0:T(8,128)} %unit0.1.x_ref, bf16[4,32,2,8,32,256]{5,4,3,2,1,0:T(8,128)(2,1)} %bitcast.47, bf16[4,32,2,8,32,256]{5,4,3,2,1,0:T(8,128)(2,1)} %bitcast.48, f32[4,1024]{1,0:T(4,128)} %bitcast.60, f32[48,256]{1,0:T(8,128)} %broadcast_in_dim.73.inside_ref, ...), custom_call_target="tpu_custom_call" | custom-call | flops 4294967296 | bytes 16777216 | tf_op jit(solution)/shard_map/unit1/pallas_call | solution.py:305
  167.2 4.0 %all-to-all-start.4 = ((bf16[4,4,64,256]{3,2,1,0:T(8,128)(2,1)}), bf16[4,4,64,256]{3,2,1,0:T(8,128)(2,1)S(1)}, u32[]{:S(2)}, u32[]{:S(2)}) async-start(bf16[4,4,64,256]{3,2,1,0:T(8,128)(2,1)} %get-tuple-element.8), calls=%async_computation.4 | async-start | bytes 1048576 | tf_op jit(solution)/shard_map/all_to_all | solution.py:423
  171.2 0.9 reshape.110
  172.4 0.9 copy.30
  173.3 7.0 %all-to-all-done.4 = bf16[4,4,64,256]{3,2,1,0:T(8,128)(2,1)S(1)} async-done(((bf16[4,4,64,256]{3,2,1,0:T(8,128)(2,1)}), bf16[4,4,64,256]{3,2,1,0:T(8,128)(2,1)S(1)}, u32[]{:S(2)}, u32[]{:S(2)}) %all-to-all-start.4) | async-done | bytes 524320 | tf_op jit(solution)/shard_map/all_to_all | solution.py:423
  180.3 6.5 %all-to-all-start.5 = ((f32[128,4,8]{2,1,0:T(4,128)}), f32[128,4,8]{2,1,0:T(4,128)S(1)}, u32[]{:S(2)}, u32[]{:S(2)}) async-start(f32[128,4,8]{2,1,0:T(4,128)} %copy.30), calls=%async_computation.5 | async-start | bytes 524288 | tf_op jit(solution)/shard_map/all_to_all | solution.py:435
  186.9 1.1 collective-permute-start.1
  188.0 9.7 %all-to-all-done.5 = f32[128,4,8]{2,1,0:T(4,128)S(1)} async-done(((f32[128,4,8]{2,1,0:T(4,128)}), f32[128,4,8]{2,1,0:T(4,128)S(1)}, u32[]{:S(2)}, u32[]{:S(2)}) %all-to-all-start.5) | async-done | bytes 16416 | tf_op jit(solution)/shard_map/all_to_all | solution.py:435
  (61 shorter events, 12.9 us)
Async XLA Ops:
  7.2 15.0 %copy-start.1 = (bf16[64,16,256]{2,1,0:T(8,128)(2,1)S(1)}, bf16[64,16,256]{2,1,0:T(8,128)(2,1)}, u32[]{:S(2)}) copy-start(bf16[64,16,256]{2,1,0:T(8,128)(2,1)} %param.14) | copy-start | bytes 1572868
  7.2 124.9 %all-gather.2.cloned.1.call-start = ((), (), s32[]{:S(2)}) async-start(), calls=%async_computation.6 | async-start | bytes 33816576 | tf_op jit(solution)/shard_map/all_gather | solution.py:371
  10.6 26.1 %all-to-all-start = ((bf16[128,16,128]{2,1,0:T(8,128)(2,1)}), bf16[128,16,128]{2,1,0:T(8,128)(2,1)S(1)}, u32[]{:S(2)}, u32[]{:S(2)}) async-start(bf16[128,16,128]{2,1,0:T(8,128)(2,1)} %broadcast_in_dim.64), calls=%async_computation | async-start | bytes 1048576 | tf_op jit(solution)/shard_map/all_to_all | solution.py:376
  24.9 1.7 copy-start.4
  24.9 1.8 copy-start.6
  24.9 1.9 copy-start.5
  24.9 2.6 %copy-start.3 = (f32[2048]{0:T(1024)S(1)}, f32[2048]{0:T(1024)}, u32[]{:S(2)}) copy-start(f32[2048]{0:T(1024)} %param.13) | copy-start | bytes 24580
  37.9 12.6 %all-to-all-start.1 = ((bf16[16,64,256]{2,1,0:T(8,128)(2,1)}), bf16[16,64,256]{2,1,0:T(8,128)(2,1)S(1)}, u32[]{:S(2)}, u32[]{:S(2)}) async-start(bf16[16,64,256]{2,1,0:T(8,128)(2,1)} %reshape.101), calls=%async_computation.1 | async-start | bytes 1048576 | tf_op jit(solution)/shard_map/all_to_all | solution.py:397
  50.5 12.5 %copy-start = (bf16[16,64,256]{2,1,0:T(8,128)(2,1)}, bf16[16,64,256]{2,1,0:T(8,128)(2,1)S(1)}, u32[]{:S(2)}) copy-start(bf16[16,64,256]{2,1,0:T(8,128)(2,1)S(1)} %all-to-all-done.1.own_ref) | copy-start | bytes 1572868
  51.1 39.6 %all-to-all-start.3 = ((f32[4,8,256]{2,1,0:T(8,128)}), f32[4,8,256]{2,1,0:T(8,128)S(1)}, u32[]{:S(2)}, u32[]{:S(2)}) async-start(f32[4,8,256]{2,1,0:T(8,128)} %broadcast_in_dim.70), calls=%async_computation.3 | async-start | bytes 65536 | tf_op jit(solution)/shard_map/all_to_all | solution.py:409
  54.9 26.0 %collective-permute-start = (bf16[16,64,256]{2,1,0:T(8,128)(2,1)S(1)}, bf16[16,64,256]{2,1,0:T(8,128)(2,1)S(1)}, u32[]{:S(2)}, u32[]{:S(2)}) collective-permute-start(bf16[16,64,256]{2,1,0:T(8,128)(2,1)S(1)} %all-to-all-done.1.own_ref), channel_id=1, source_target_pairs={{0,1},{1,0},{2,3},{3,2},{4,5},{5,4},{6,7},{7,6},{8,9},{9,8},{10,11... | collective-permute-start | bytes 1572872 | tf_op jit(solution)/shard_map/ppermute | solution.py:398
  80.9 0.8 copy-start.2
  90.8 29.7 %all-to-all-start.2 = ((bf16[64,48,128]{2,1,0:T(8,128)(2,1)}), bf16[64,48,128]{2,1,0:T(8,128)(2,1)S(1)}, u32[]{:S(2)}, u32[]{:S(2)}) async-start(bf16[64,48,128]{2,1,0:T(8,128)(2,1)} %upsample.1), calls=%async_computation.2 | async-start | bytes 1572864 | tf_op jit(solution)/shard_map/all_to_all | solution.py:404
  167.2 13.1 %all-to-all-start.4 = ((bf16[4,4,64,256]{3,2,1,0:T(8,128)(2,1)}), bf16[4,4,64,256]{3,2,1,0:T(8,128)(2,1)S(1)}, u32[]{:S(2)}, u32[]{:S(2)}) async-start(bf16[4,4,64,256]{3,2,1,0:T(8,128)(2,1)} %get-tuple-element.8), calls=%async_computation.4 | async-start | bytes 1048576 | tf_op jit(solution)/shard_map/all_to_all | solution.py:423
  180.3 17.4 %all-to-all-start.5 = ((f32[128,4,8]{2,1,0:T(4,128)}), f32[128,4,8]{2,1,0:T(4,128)S(1)}, u32[]{:S(2)}, u32[]{:S(2)}) async-start(f32[128,4,8]{2,1,0:T(4,128)} %copy.30), calls=%async_computation.5 | async-start | bytes 524288 | tf_op jit(solution)/shard_map/all_to_all | solution.py:435
  186.9 11.6 %collective-permute-start.1 = (bf16[2,4,64,256]{3,2,1,0:T(8,128)(2,1)S(1)}, bf16[2,4,64,256]{3,2,1,0:T(8,128)(2,1)S(1)}, u32[]{:S(2)}, u32[]{:S(2)}) collective-permute-start(bf16[2,4,64,256]{3,2,1,0:T(8,128)(2,1)S(1)} %constant_dynamic-slice_fusion), channel_id=1, source_target_pairs={{0,1},{1,0},{2,3},{3,2},{4,5},{5,4},{6,7},{7,6},{8,9},{9,8},{10,11... | collective-permute-start | bytes 786440 | tf_op jit(solution)/shard_map/ppermute | solution.py:427
Sparse Core Ops, SparseCore 0:
  11.0 121.0 all-gather.1

commit v2 on v0

v2 whole, which is shorter than its diff:
```python
import functools
import math

import jax
import jax.numpy as jnp
from jax import lax
from jax.experimental import pallas as pl
from jax.experimental.pallas import tpu as pltpu
from jax.sharding import Mesh
from jax.sharding import PartitionSpec as P

BF = jnp.bfloat16
F32 = jnp.float32
SIN2 = (
    9.869603157043457,
    -32.469581604003906,
    42.72538375854492,
    -30.085952758789062,
    12.990730285644531,
    -3.2729458808898926,
)
ROW_CHUNK = 512
EDGE = 2
VMEM = 60 * 1024 * 1024


def snake(value, turns, inverse):
    u = value * turns
    r = u - jnp.round(u)
    z = r * r
    p = jnp.full_like(z, SIN2[-1])
    for coefficient in SIN2[-2::-1]:
        p = p * z + coefficient
    return value + (p * z) * inverse


def front_kernel(slots, info_ref, lat_ref, w_in_ref, freq_ref, own_ref, other_ref, out_ref, w_s, one_s, two_s, prod_s, x_s):
    step, steps = pl.program_id(0), pl.num_programs(0)
    groups, depth, cols = own_ref.shape
    half = cols // 2
    _, frames, lanes = lat_ref.shape
    width = lanes // 2
    reach = w_in_ref.shape[0] // width // 2
    rows = frames * slots

    @pl.when(step == 0)
    def _():
        column = lax.broadcasted_iota(jnp.int32, (frames, lanes), 1)
        frame = lax.broadcasted_iota(jnp.int32, (frames, lanes), 0)
        edge = reach * slots
        one_s[0:edge, :] = jnp.zeros((edge, lanes), F32)
        one_s[edge + rows :, :] = jnp.zeros((one_s.shape[0] - edge - rows, lanes), F32)
        for k in range(slots):
            clip = info_ref[2 + k]
            v = lat_ref[lax.div(clip, 2)].astype(F32)
            v = jnp.where(lax.rem(clip, 2) == 1, pltpu.roll(v, width, 1), v)
            keep = (column < width) & (frame < info_ref[2 + slots + k])
            one_s[pl.ds(edge + k, frames, stride=slots), :] = jnp.where(keep, v, 0.0)
        total = two_s.shape[0]
        for r in range(0, total, ROW_CHUNK):
            size = min(ROW_CHUNK, total - r)
            after = pltpu.roll(one_s[r + slots : r + slots + size, :], width, 1)
            two_s[r : r + size, :] = one_s[r : r + size, :] + after

        first, second = (own_ref, other_ref), (other_ref, own_ref)
        for core, pair in enumerate((first, second)):

            @pl.when(info_ref[0] == core)
            def _(pair=pair):
                for g in range(groups):
                    for c in range(2):
                        w_s[(2 * g + c) * depth : (2 * g + c + 1) * depth, :] = pair[c][g]

        prod_s[0:8, :] = jnp.zeros((8, cols), F32)
        prod_s[prod_s.shape[0] - 8 :, :] = jnp.zeros((8, cols), F32)

    at = pl.multiple_of(step * ROW_CHUNK, ROW_CHUNK)
    taps = 2 * reach + 1
    lhs = []
    for t in range(0, taps, 2):
        v = two_s[pl.ds(pl.multiple_of(at + t * slots, 8), ROW_CHUNK), :].astype(BF)
        lhs.append(v if t + 1 < taps else v[:, :width])
    lhs = jnp.concatenate(lhs, axis=1)
    total = None
    block = 512
    for n in range(w_in_ref.shape[1] // block):
        part = slice(n * block, (n + 1) * block)
        pre = jnp.dot(lhs, w_in_ref[:, part], preferred_element_type=F32)
        s0 = snake(pre, freq_ref[0:1, part], freq_ref[1:2, part]).astype(BF)
        term = jnp.dot(s0, w_s[part, :], preferred_element_type=F32)
        total = term if total is None else total + term
    prod_s[pl.ds(pl.multiple_of(8 + at, 8), ROW_CHUNK), :] = total

    @pl.when(step == steps - 1)
    def _():
        pad = EDGE * slots
        x_s[0:pad, :] = jnp.zeros((pad, half), F32)
        x_s[x_s.shape[0] - pad :, :] = jnp.zeros((pad, half), F32)
        low = info_ref[1] == 0
        for r in range(0, rows, ROW_CHUNK):
            centre = prod_s[8 + r : 8 + r + ROW_CHUNK, :half]
            before = prod_s[8 - slots + r : 8 - slots + r + ROW_CHUNK, half:]
            after = prod_s[8 + slots + r : 8 + slots + r + ROW_CHUNK, half:]
            x_s[pad + r : pad + r + ROW_CHUNK, :] = centre + jnp.where(low, before, after)
        window = out_ref.shape[1]
        kept = window - 2 * pad
        for d in range(out_ref.shape[0]):
            out_ref[d] = x_s[d * kept : d * kept + window, :].astype(BF)


def activate_kernel(slots, x_ref, freq_ref, out_ref, act_s):
    phases, halves, groups, rows, lanes = x_ref.shape
    for s in range(phases):
        act_s[s, 0:8, :] = jnp.zeros((8, act_s.shape[2]), F32)
        act_s[s, 8 + rows :, :] = jnp.zeros((8, act_s.shape[2]), F32)
        for g in range(groups):
            for h in range(halves):
                cols = slice((g * halves + h) * lanes, (g * halves + h + 1) * lanes)
                v = x_ref[s, h, g].astype(F32)
                act_s[s, 8 : 8 + rows, cols] = snake(v, freq_ref[0, 0:1, cols], freq_ref[0, 1:2, cols])
    reach = (out_ref.shape[0] - phases) // 2
    for i in range(out_ref.shape[0]):
        n = i - reach
        at = 8 + n // phases * slots
        out_ref[i] = act_s[n % phases, at : at + rows, :].astype(BF)


def units_kernel(
    slots,
    info_ref,
    a0_ref,
    x_ref,
    freq_ref,
    w_ref,
    *refs,
):
    phases, halves, groups, rows, lanes = x_ref.shape
    dec_refs = refs[:groups]
    near_ref, far_ref, w_s, p_s, act_s, a1_s, x1_s, acc_s, b_s, t_s, o_s, w_sem, p_sem = refs[groups:]
    taps = w_s.shape[2]
    width = halves * lanes
    channels = groups * width
    first = EDGE * slots
    kept = rows - 2 * first
    frames = kept // slots
    units = w_sem.shape[0] // groups

    def fetch(unit):
        for g in range(groups):
            i = unit * groups + g
            yield pltpu.make_async_copy(w_ref.at[g, :, unit * taps : (unit + 1) * taps], w_s.at[i], w_sem.at[i])
        yield pltpu.make_async_copy(w_ref.at[:, :, units * taps + unit], p_s.at[unit], p_sem.at[unit])

    for copy in list(fetch(0))[: groups // 2]:
        copy.start()

    row = lax.broadcasted_iota(jnp.int32, (rows, lanes), 0)
    at = info_ref[0] - EDGE + (row >> (slots.bit_length() - 1))
    inside = jnp.where((at >= 0) & (at < info_ref[1]), 1.0, 0.0).astype(F32)
    row = lax.broadcasted_iota(jnp.int32, (kept, lanes), 0)
    at = info_ref[0] + (row >> (slots.bit_length() - 1))
    slot = row & (slots - 1)
    limit = jnp.zeros((kept, lanes), jnp.int32)
    for k in range(slots):
        limit = jnp.where(slot == k, info_ref[4 + k], limit)
    live = jnp.where(at < limit, 1.0, 0.0).astype(F32)

    for s in range(phases):
        act_s[s, 0:8, :] = jnp.zeros((8, channels), F32)
        act_s[s, 8 + rows :, :] = jnp.zeros((8, channels), F32)

    for unit in range(units):
        a_ref = a0_ref if unit == 0 else a1_s
        dilation = 3**unit
        m = phases * a_ref.shape[1]
        copies = list(fetch(unit))
        ahead = list(fetch(unit + 1)) if unit + 1 < units else []
        split = groups // 2 if unit == 0 else len(copies)
        for copy in copies[:split]:
            copy.wait()
        for copy in copies[split:] + ([] if unit == 0 else ahead):
            copy.start()
        for g in range(groups):
            if unit == 0 and g == split:
                for copy in copies[split:]:
                    copy.wait()
                for copy in ahead:
                    copy.start()
            total = None
            for t in range(taps):
                lhs = a_ref[dilation * t : dilation * t + phases].reshape(m, channels)
                rhs = w_s[unit * groups + g, :, t].reshape(channels, width)
                term = jnp.dot(lhs, rhs, preferred_element_type=F32)
                total = term if total is None else total + term
            acc_s[g % 2, 0:m] = total
            cols = slice(g * width, (g + 1) * width)
            b_s[0:m, cols] = snake(
                acc_s[g % 2, 0:m], freq_ref[unit, 2:3, cols], freq_ref[unit, 3:4, cols]
            ).astype(BF)
        if unit == 0:
            for g in range(groups):
                acc = acc_s.at[g % 2]
                acc[0:m] = jnp.dot(b_s[0:m], p_s[unit, g].reshape(channels, width), preferred_element_type=F32)
                for s in range(phases):
                    for h in range(halves):
                        cols = slice(g * width + h * lanes, g * width + (h + 1) * lanes)
                        v = acc[s * rows : (s + 1) * rows, h * lanes : (h + 1) * lanes]
                        v = v + x_ref[s, h, g].astype(F32)
                        x1_s[s, :, cols] = v[first : first + kept]
                        act_s[s, 8 : 8 + rows, cols] = (
                            snake(v, freq_ref[1, 0:1, cols], freq_ref[1, 1:2, cols]) * inside
                        )
            reach = (a1_s.shape[0] - phases) // 2
            for i in range(a1_s.shape[0]):
                n = i - reach
                at = 8 + first + n // phases * slots
                a1_s[i] = act_s[n % phases, at : at + kept, :].astype(BF)
            continue
        for order in range(groups):
            g = lax.rem(info_ref[2] + order, groups)
            acc = acc_s.at[order % 2]
            acc[0:m] = jnp.dot(b_s[0:m], p_s[unit, g].reshape(channels, width), preferred_element_type=F32)
            for h in range(halves):
                inner = slice(h * lanes, (h + 1) * lanes)
                cols = pl.ds(pl.multiple_of(g * width + h * lanes, lanes), lanes)
                squares = jnp.zeros((kept, lanes), F32)
                for s in range(phases):
                    v = acc[s * kept : (s + 1) * kept, inner] + x1_s[s, :, cols]
                    squares += v * v * live
                    t_s[...] = v
                    for k in range(slots):
                        o_s[pl.ds(k * frames * phases + s, frames, stride=phases), :] = t_s[
                            pl.ds(k, frames, stride=slots), :
                        ]
                t_s[...] = squares
                sums = sum(t_s[f * slots : (f + 1) * slots, :] for f in range(frames))
                share = near_ref.shape[2]
                for j in range(0, lanes // share, 2):
                    even = sums if j == 0 else pltpu.roll(sums, lanes - j * share, 1)
                    odd = pltpu.roll(sums, lanes - (j + 1) * share, 1)
                    chip = lax.div(g * (width // share) + h * (lanes // share) + j, 2)
                    near_ref[chip] = jnp.where(info_ref[3] == 0, even, odd)[:, :share]
                    far_ref[chip] = jnp.where(info_ref[3] == 0, odd, even)[:, :share]
                for k in range(slots):
                    dec_refs[order][k, :, inner] = o_s[k * frames * phases : (k + 1) * frames * phases, :].astype(BF)


def place_kernel(info_ref, *refs):
    pieces, out_ref = refs[:-1], refs[-1]
    slots, samples, _ = pieces[0].shape
    for k, piece in enumerate(pieces):
        r = lax.rem(info_ref[0] - k + len(pieces), len(pieces))
        at = pl.multiple_of(lax.div(r, 2) * samples, samples)
        out_ref[pl.ds(lax.rem(r, 2) * slots, slots), pl.ds(at, samples), :] = piece[...]


def cost(flops, moved):
    return pl.CostEstimate(flops=flops, bytes_accessed=moved, transcendentals=0)


def run_pack(first, second):
    n = first.shape[0]

    def pack_kernel(first_ref, second_ref, out_ref):
        out_ref[0:n] = first_ref[...]
        out_ref[n:] = second_ref[...]

    return pl.pallas_call(
        pack_kernel,
        out_shape=jax.ShapeDtypeStruct((n + second.shape[0], *first.shape[1:]), first.dtype),
        compiler_params=pltpu.CompilerParams(vmem_limit_bytes=VMEM // 4),
        cost_estimate=cost(0, 4 * (first.size + second.size)),
        name="pack",
    )(first, second)


def run_front(info, lat, w_in, freq, own, other, slots, chips):
    groups, frames, lanes = lat.shape
    c0 = w_in.shape[1]
    cols = own.shape[2]
    half = cols // 2
    rows = frames * slots
    pad = EDGE * slots
    window = rows // chips + 2 * pad
    reach = w_in.shape[0] // (lanes // 2) // 2
    whole = pl.BlockSpec(own.shape, lambda i: (0, 0, 0))
    return pl.pallas_call(
        functools.partial(front_kernel, slots),
        grid=(rows // ROW_CHUNK,),
        in_specs=[
            pl.BlockSpec(memory_space=pltpu.SMEM),
            pl.BlockSpec(lat.shape, lambda i: (0, 0, 0)),
            pl.BlockSpec(w_in.shape, lambda i: (0, 0)),
            pl.BlockSpec(freq.shape, lambda i: (0, 0)),
            whole,
            whole,
        ],
        out_specs=pl.BlockSpec((chips, window, half), lambda i: (0, 0, 0)),
        out_shape=jax.ShapeDtypeStruct((chips, window, half), BF),
        scratch_shapes=[
            pltpu.VMEM((c0, cols), BF),
            pltpu.VMEM((rows + (2 * reach + 2) * slots, lanes), F32),
            pltpu.VMEM((rows + 2 * reach * slots, lanes), F32),
            pltpu.VMEM((rows + 16, cols), F32),
            pltpu.VMEM((rows + 2 * pad, half), F32),
        ],
        compiler_params=pltpu.CompilerParams(vmem_limit_bytes=VMEM),
        cost_estimate=cost(2 * rows * c0 * (w_in.shape[0] + cols), 2 * w_in.size),
        name="front",
    )(info, lat, w_in, freq, own, other)


def run_activate(x, freq, slots, reach):
    phases, halves, groups, rows, lanes = x.shape
    channels = groups * halves * lanes
    return pl.pallas_call(
        functools.partial(activate_kernel, slots),
        out_shape=jax.ShapeDtypeStruct((phases + 2 * reach, rows, channels), BF),
        scratch_shapes=[pltpu.VMEM((phases, rows + 16, channels), F32)],
        compiler_params=pltpu.CompilerParams(vmem_limit_bytes=VMEM),
        cost_estimate=cost(20 * x.size, 6 * x.size),
        name="activate",
    )(x, freq)


def run_units(info, act, x, freq, weights, slots, devices):
    phases, halves, groups, rows, lanes = x.shape
    _, shards, kinds, depth, width = weights.shape
    units = freq.shape[0]
    taps = kinds // units - 1
    kept = rows - 2 * EDGE * slots
    channels = groups * width
    m = phases * kept
    reach = taps // 2 * 3 ** (units - 1)
    vmem = pl.BlockSpec(memory_space=pltpu.VMEM)
    return pl.pallas_call(
        functools.partial(units_kernel, slots),
        in_specs=[
            pl.BlockSpec(memory_space=pltpu.SMEM),
            vmem,
            vmem,
            vmem,
            pl.BlockSpec(memory_space=pl.ANY),
        ],
        out_specs=[vmem] * (groups + 2),
        out_shape=[
            *[jax.ShapeDtypeStruct((slots, m // slots, width), BF)] * groups,
            *[jax.ShapeDtypeStruct((devices // 2, slots, channels // devices), F32)] * 2,
        ],
        scratch_shapes=[
            pltpu.VMEM((units * groups, shards, taps, depth, width), BF),
            pltpu.VMEM((units, groups, shards, depth, width), BF),
            pltpu.VMEM((phases, rows + 16, channels), F32),
            pltpu.VMEM((phases + 2 * reach, kept, channels), BF),
            pltpu.VMEM((phases, kept, channels), F32),
            pltpu.VMEM((2, phases * rows, width), F32),
            pltpu.VMEM((phases * rows, channels), BF),
            pltpu.VMEM((kept, lanes), F32),
            pltpu.VMEM((m, lanes), F32),
            pltpu.SemaphoreType.DMA((units * groups,)),
            pltpu.SemaphoreType.DMA((units,)),
        ],
        compiler_params=pltpu.CompilerParams(vmem_limit_bytes=VMEM),
        cost_estimate=cost((phases * rows + m) * kinds * channels * channels, 2 * weights.size),
        name="units",
    )(info, act, x, freq, weights)


def run_place(place, pieces):
    slots, samples, width = pieces[0].shape
    vmem = pl.BlockSpec(memory_space=pltpu.VMEM)
    return pl.pallas_call(
        place_kernel,
        in_specs=[pl.BlockSpec(memory_space=pltpu.SMEM), *[vmem] * len(pieces)],
        out_specs=vmem,
        out_shape=jax.ShapeDtypeStruct((2 * slots, len(pieces) // 2 * samples, width), pieces[0].dtype),
        compiler_params=pltpu.CompilerParams(vmem_limit_bytes=VMEM // 4),
        cost_estimate=cost(0, 4 * len(pieces) * pieces[0].size),
        name="place",
    )(place, *pieces)


def freq_rows(alpha):
    return jnp.stack([alpha / math.pi, 1.0 / alpha], axis=-2)


def body(
    latent,
    dest,
    lengths,
    input_conv_weight,
    snake_entry_frequency,
    upsample_weight,
    snake_unit_frequency,
    dilated_conv_weight,
    pointwise_conv_weight,
):
    everyone = ("y", "x", "z", "c")
    blocks = ("x", "z", "y")
    ny, nx, nz, nc = (lax.axis_size(a) for a in everyone)
    iy, ix, iz, ic = (lax.axis_index(a) for a in everyone)
    chips = ny * nx * nz
    here_clips, here_frames, width_in = latent.shape
    clips = dest.shape[0]
    frames = here_frames * nx * nz * nc
    slots = clips // nc
    own_frames = frames // chips
    units, taps = dilated_conv_weight.shape[:2]
    upk, c1_local = upsample_weight.shape[1:]
    phases = upk // 2
    halves = nx * nz // phases
    lanes = c1_local // halves
    first_slot = ic * slots

    weights = run_pack(dilated_conv_weight.reshape(-1, *dilated_conv_weight.shape[2:]), pointwise_conv_weight)
    kinds = weights.shape[0]
    weights = lax.all_gather(weights, everyone, axis=0, tiled=True)
    weights = weights.reshape(ny, nx * nz * nc, kinds, *weights.shape[1:])

    packed = latent.transpose(1, 0, 2).reshape(here_frames, here_clips * width_in)
    packed = jnp.broadcast_to(packed[None], (ny * nx * nz * nc,) + packed.shape)
    packed = lax.all_to_all(packed, everyone, 0, 0, tiled=True)
    my_dest = lax.dynamic_slice_in_dim(dest, first_slot, slots)
    my_lengths = lax.dynamic_slice_in_dim(lengths, first_slot, slots)

    order = []
    for s in range(phases):
        near = s + phases // 2
        far = s + 3 * phases // 2 if s < phases // 2 else s - phases // 2
        order += [near, far]
    up = upsample_weight.transpose(1, 0, 2)
    up = jnp.stack([up[q] for q in order]).reshape(phases, 2, -1, halves, lanes)
    up = up.transpose(0, 3, 2, 1, 4).reshape(phases * halves, -1, 2 * lanes)
    up, packed = lax.optimization_barrier((up, packed))
    own = lax.all_to_all(up, ("x", "z"), 0, 0, tiled=True)
    other = lax.ppermute(own, "c", [(i, nc - 1 - i) for i in range(nc)])

    w_in = input_conv_weight.reshape(-1, input_conv_weight.shape[2])
    info = jnp.stack([ic, (ix * nz + iz) // (phases // 2 * halves)])
    info = jnp.concatenate([info, my_dest, my_lengths]).astype(jnp.int32)
    packed = packed.reshape(ny, frames, here_clips * width_in)
    x = run_front(info, packed, w_in, freq_rows(snake_entry_frequency), own, other, slots, chips)
    x = lax.all_to_all(x, blocks, 0, 0, tiled=True)
    x = x.reshape(phases, halves, ny, x.shape[1], lanes)

    freq = freq_rows(snake_unit_frequency).reshape(1, -1, c1_local)
    freq = lax.all_to_all(jnp.broadcast_to(freq, (ny,) + freq.shape[1:]), "y", 0, 0, tiled=True)
    freq = freq.transpose(1, 0, 2).reshape(units, -1, ny * c1_local)

    block = (ix * nz + iz) * ny + iy
    start = 2 * (iy % 2) + ic
    info = jnp.concatenate([jnp.stack([block * own_frames, frames, start, ic]), my_lengths]).astype(jnp.int32)
    act = run_activate(x, freq, slots, taps // 2)
    *decoded, near, far = run_units(info, act, x, freq, weights, slots, ny * nx * nz * nc)

    far = lax.ppermute(far, "c", [(i, nc - 1 - i) for i in range(nc)])
    squares = lax.all_to_all(jnp.concatenate([near, far], axis=1), ("y", "x", "z"), 0, 0, tiled=True)

    pieces = []
    for k, piece in enumerate(decoded):
        pairs = []
        for y in range(ny):
            for c in range(nc):
                target = (2 * (y % 2) + c + k) % ny
                pairs.append((y * nc + c, target * nc + y // 2))
        pieces.append(lax.ppermute(piece, ("y", "c"), pairs))
    decoded = run_place(iy[None].astype(jnp.int32), pieces)

    squares = squares.sum(axis=0)
    squares = jnp.where(ic == 0, squares, jnp.roll(squares, slots, axis=0))
    count = (phases * lengths[:, None]).astype(F32)
    energy = jnp.log(squares / count + 1e-06)
    return decoded, energy


def solution(mesh):
    ny = mesh.shape["clip"]
    side = 4
    fine = Mesh(mesh.devices.reshape(ny, side, side, 2), ("y", "x", "z", "c"))
    tm = ("x", "z", "c")
    in_specs = (
        P("y", tm, None),
        P(),
        P(),
        P(),
        P(),
        P(tm, None, "y"),
        P(None, None, "y"),
        P(None, None, tm, "y"),
        P(None, tm, "y"),
    )
    out_specs = (P(None, tm, "y"), P(None, ("y",) + tm))
    return jax.shard_map(body, mesh=fine, in_specs=in_specs, out_specs=out_specs, check_vma=False)
```

time: 433 us -> 188 us (0.43)
  blocking collectives: 128 us -> 0 us
  waiting for transfers between devices: 175 us -> 66.1 us
  matrix products: 47.5 us -> 0 us
  Pallas kernels: 0 us -> 41.8 us
  starting transfers between devices: 25.1 us -> 49.4 us
  local copies, waits for them, and re-layouts: 29.5 us -> 11.6 us
  other arithmetic: 9.07 us -> 3.74 us
    all_gather x7 -> x1, waiting for transfers between devices: 164 us -> 22.7 us  [body(): weights = lax.all_gather(weights, everyone, axis=0, tiled=True)]
    unnamed x1 -> x0, blocking collectives: 64.7 us -> none
    all_gather x3 -> x0, blocking collectives: 63.3 us -> none  [the longest x2 52.7 us: body(): lax.all_gather(pointwise_conv_weight[residual_unit], 'tm', axis=0, tiled=...]
    dot_general x24 -> x0, matrix products: 47.5 us -> none  [the longest x21 29.3 us: kernel_tap_count(): jnp.einsum('cli,io->clo', replay_window, weight_bundle[kernel_tap], prefe...]
    pallas_call x0 -> x5, Pallas kernels: none -> 41.8 us  [the longest x1 20.7 us: run_units(): pl.pallas_call(functools.partial(units_kernel, slots), in_specs=[pl.Block...]
    all_to_all x0 -> x5, waiting for transfers between devices: none -> 39.9 us  [the longest x1 21 us: body(): x = lax.all_to_all(x, blocks, 0, 0, tiled=True)]
    all_to_all x0 -> x5, starting transfers between devices: none -> 34 us  [the longest x1 11.5 us: body(): packed = lax.all_to_all(packed, everyone, 0, 0, tiled=True)]
    reshape x1 -> x4, local copies, waits for them, and re-layouts: 24.1 us -> 2.32 us  [the longest x1 1.16 us: body(): up = up.transpose(0, 3, 2, 1, 4).reshape(phases * halves, -1, 2 * lanes)]
  transfers between devices with their start and end apart: 15 -> 12, of which waited for: 10 -> 8; matrix products, arithmetic and copies ran while one was open for 13% -> 5% of each run, Pallas kernels for 0% -> 10%
where the time goes in v2:
time: 188 us; the launch traced here: 187 us
  waiting for transfers between devices  66.1 us (35%)
  starting transfers between devices  49.4 us (26%)
  Pallas kernels  41.8 us (22%)
  between operations  14.3 us (8%)
  local copies, waits for them, and re-layouts  11.6 us (6%)
  other arithmetic  3.74 us (2%)
    all_gather x1, waiting for transfers between devices, body(): weights = lax.all_gather(weights, everyone, axis=0, tiled=True)  22.7 us
    all_to_all x1, waiting for transfers between devices, body(): x = lax.all_to_all(x, blocks, 0, 0, tiled=True)  21 us
    pallas_call x1, Pallas kernels, run_units(): pl.pallas_call(functools.partial(units_kernel, slots), in_specs=[pl.Block...  20.7 us
    pallas_call x1, Pallas kernels, run_front(): pl.pallas_call(functools.partial(front_kernel, slots), grid=(rows // ROW_...  16.3 us
    ppermute x4, starting transfers between devices, body(): pieces.append(lax.ppermute(piece, ('y', 'c'), pairs))  12 us
    all_to_all x1, starting transfers between devices, body(): packed = lax.all_to_all(packed, everyone, 0, 0, tiled=True)  11.5 us
    all_to_all x1, waiting for transfers between devices, body(): packed = lax.all_to_all(packed, everyone, 0, 0, tiled=True)  10.3 us
    all_to_all x1, waiting for transfers between devices, body(): own = lax.all_to_all(up, ('x', 'z'), 0, 0, tiled=True)  8.7 us
  transfers between devices with their start and end apart: 12, of which 8 were waited for; matrix products, arithmetic and copies ran while one was open for 5% of the time, Pallas kernels for 10%

profile of v2, /device:TPU:1, one launch (start us, length us, event | category | flops | bytes accessed | tf_op | source)
XLA Modules:
  0.0 187.1 jit_solution(6389450927184431307)
XLA Ops:
  7.2 0.9 copy-done
  8.2 0.8 copy-done.1
  8.9 0.7 pack.1
  9.6 0.7 copy.29
  10.4 0.9 broadcast_in_dim.20
  11.3 11.5 %all-to-all-start = ((bf16[128,16,128]{2,1,0:T(8,128)(2,1)}), bf16[128,16,128]{2,1,0:T(8,128)(2,1)S(1)}, u32[]{:S(2)}, u32[]{:S(2)}) async-start(bf16[128,16,128]{2,1,0:T(8,128)(2,1)} %broadcast_in_dim.20), calls=%async_computation | async-start | bytes 1048576 | tf_op jit(solution)/shard_map/all_to_all | solution.py:422
  22.8 1.1 fusion.3
  23.9 1.6 stack.38
  26.2 1.2 reshape.35
  27.3 10.3 %all-to-all-done = bf16[128,16,128]{2,1,0:T(8,128)(2,1)S(1)} async-done(((bf16[128,16,128]{2,1,0:T(8,128)(2,1)}), bf16[128,16,128]{2,1,0:T(8,128)(2,1)S(1)}, u32[]{:S(2)}, u32[]{:S(2)}) %all-to-all-start) | async-done | bytes 524320 | tf_op jit(solution)/shard_map/all_to_all | solution.py:422
  37.6 3.6 %all-to-all-start.1 = ((bf16[16,64,256]{2,1,0:T(8,128)(2,1)}), bf16[16,64,256]{2,1,0:T(8,128)(2,1)S(1)}, u32[]{:S(2)}, u32[]{:S(2)}) async-start(bf16[16,64,256]{2,1,0:T(8,128)(2,1)} %reshape.35), calls=%async_computation.1 | async-start | bytes 1048576 | tf_op jit(solution)/shard_map/all_to_all | solution.py:435
  41.4 8.7 %all-to-all-done.1.own_ref = bf16[16,64,256]{2,1,0:T(8,128)(2,1)S(1)} async-done(((bf16[16,64,256]{2,1,0:T(8,128)(2,1)}), bf16[16,64,256]{2,1,0:T(8,128)(2,1)S(1)}, u32[]{:S(2)}, u32[]{:S(2)}) %all-to-all-start.1) | async-done | bytes 524320 | tf_op jit(solution)/shard_map/all_to_all | solution.py:435
  50.8 3.8 %all-to-all-start.3 = ((f32[4,8,256]{2,1,0:T(8,128)}), f32[4,8,256]{2,1,0:T(8,128)S(1)}, u32[]{:S(2)}, u32[]{:S(2)}) async-start(f32[4,8,256]{2,1,0:T(8,128)} %broadcast_in_dim.22), calls=%async_computation.3 | async-start | bytes 65536 | tf_op jit(solution)/shard_map/all_to_all | solution.py:447
  54.5 3.1 %collective-permute-start = (bf16[16,64,256]{2,1,0:T(8,128)(2,1)S(1)}, bf16[16,64,256]{2,1,0:T(8,128)(2,1)S(1)}, u32[]{:S(2)}, u32[]{:S(2)}) collective-permute-start(bf16[16,64,256]{2,1,0:T(8,128)(2,1)S(1)} %all-to-all-done.1.own_ref), channel_id=1, source_target_pairs={{0,1},{1,0},{2,3},{3,2},{4,5},{5,4},{6,7},{7,6},{8,9},{9,8},{10,11... | collective-permute-start | bytes 1572872 | tf_op jit(solution)/shard_map/ppermute | solution.py:436
  57.6 0.7 pad_add_fusion.info_ref
  59.2 0.8 copy-done.8
  60.0 16.3 %front.1 = bf16[64,48,128]{2,1,0:T(8,128)(2,1)} custom-call(s32[10]{0:T(128)} %pad_add_fusion.info_ref, bf16[4,512,128]{2,1,0:T(8,128)(2,1)} %bitcast.29, bf16[448,2048]{1,0:T(8,128)(2,1)} %bitcast.35, f32[2,2048]{1,0:T(2,128)} %pad_maximum_fusion.1.freq_ref, bf16[16,64,256]{2,1,0:T(8,128)(2,1)} %copy-done.5, bf16[16,64,256]{2,1,0:T(8,128)(2,1)} %copy-done.8), custom_call_target="tpu_custom_call" | custom-call | flops 5905580032 | bytes 1835008 | tf_op jit(solution)/shard_map/front/pallas_call | solution.py:287
  76.3 7.0 %all-to-all-start.2 = ((bf16[64,48,128]{2,1,0:T(8,128)(2,1)}), bf16[64,48,128]{2,1,0:T(8,128)(2,1)S(1)}, u32[]{:S(2)}, u32[]{:S(2)}) async-start(bf16[64,48,128]{2,1,0:T(8,128)(2,1)} %front.1), calls=%async_computation.2 | async-start | bytes 1572864 | tf_op jit(solution)/shard_map/all_to_all | solution.py:443
  84.7 21.0 %all-to-all-done.2 = bf16[64,48,128]{2,1,0:T(8,128)(2,1)S(1)} async-done(((bf16[64,48,128]{2,1,0:T(8,128)(2,1)}), bf16[64,48,128]{2,1,0:T(8,128)(2,1)S(1)}, u32[]{:S(2)}, u32[]{:S(2)}) %all-to-all-start.2) | async-done | bytes 786464 | tf_op jit(solution)/shard_map/all_to_all | solution.py:443
  105.6 0.9 copy-done.2
  106.5 3.3 %activate.1.a0_ref = bf16[14,48,1024]{2,1,0:T(8,128)(2,1)} custom-call(bf16[8,2,4,48,128]{4,3,2,1,0:T(8,128)(2,1)} %bitcast.25, f32[2,4,1024]{2,1,0:T(4,128)} %reshape.39.freq_ref), custom_call_target="tpu_custom_call" | custom-call | flops 7864320 | bytes 2359296 | tf_op jit(solution)/shard_map/activate/pallas_call | solution.py:316
  109.9 22.7 %all-gather.2.cloned.1.call-done = bf16[2048,32,256]{2,1,0:T(8,128)(2,1)} async-done(((bf16[16,32,256]{2,1,0:T(8,128)(2,1)}), bf16[2048,32,256]{2,1,0:T(8,128)(2,1)}) %all-gather.2.cloned.1.call-update) | async-done | bytes 33554448 | tf_op jit(solution)/shard_map/all_gather | solution.py:417
  132.6 20.7 %units.1 = (bf16[4,64,256]{2,1,0:T(8,128)(2,1)}, bf16[4,64,256]{2,1,0:T(8,128)(2,1)}, bf16[4,64,256]{2,1,0:T(8,128)(2,1)}, bf16[4,64,256]{2,1,0:T(8,128)(2,1)}, ...) custom-call(s32[8]{0:T(128)} %concatenate.13.info_ref, bf16[14,48,1024]{2,1,0:T(8,128)(2,1)} %activate.1.a0_ref, ...), custom_call_target="tpu_custom_call" | custom-call | flops 10737418240 | bytes 33554432 | tf_op jit(solution)/shard_map/units/pallas_call | solution.py:336
  153.6 1.3 collective-permute-done.5
  154.9 1.7 pad_maximum_fusion
  156.6 8.1 %all-to-all-start.4 = ((f32[64,8,8]{2,1,0:T(8,128)}), f32[64,8,8]{2,1,0:T(8,128)S(1)}, u32[]{:S(2)}, u32[]{:S(2)}) async-start(f32[64,8,8]{2,1,0:T(8,128)} %pad_maximum_fusion), calls=%async_computation.4 | async-start | bytes 524288 | tf_op jit(solution)/shard_map/all_to_all | solution.py:457
  164.7 3.6 %collective-permute-start.1 = (bf16[4,64,256]{2,1,0:T(8,128)(2,1)}, bf16[4,64,256]{2,1,0:T(8,128)(2,1)S(1)}, u32[]{:S(2)}, u32[]{:S(2)}) collective-permute-start(bf16[4,64,256]{2,1,0:T(8,128)(2,1)} %get-tuple-element.12), channel_id=1, source_target_pairs={{0,0},{1,32},{32,64},{33,96},{64,1},{65,33},{96,65},{97,97},{2,2},... | collective-permute-start | bytes 393224 | tf_op jit(solution)/shard_map/ppermute | solution.py:466
  168.3 3.5 %collective-permute-start.2 = (bf16[4,64,256]{2,1,0:T(8,128)(2,1)}, bf16[4,64,256]{2,1,0:T(8,128)(2,1)S(1)}, u32[]{:S(2)}, u32[]{:S(2)}) collective-permute-start(bf16[4,64,256]{2,1,0:T(8,128)(2,1)} %get-tuple-element.13), channel_id=1, source_target_pairs={{0,32},{1,64},{32,96},{33,0},{64,33},{65,65},{96,97},{97,1},{2,34}... | collective-permute-start | bytes 393224 | tf_op jit(solution)/shard_map/ppermute | solution.py:466
  171.9 4.7 %collective-permute-start.4 = (bf16[4,64,256]{2,1,0:T(8,128)(2,1)}, bf16[4,64,256]{2,1,0:T(8,128)(2,1)S(1)}, u32[]{:S(2)}, u32[]{:S(2)}) collective-permute-start(bf16[4,64,256]{2,1,0:T(8,128)(2,1)} %get-tuple-element.15), channel_id=1, source_target_pairs={{0,96},{1,0},{32,32},{33,64},{64,97},{65,1},{96,33},{97,65},{2,98}... | collective-permute-start | bytes 393224 | tf_op jit(solution)/shard_map/ppermute | solution.py:466
  176.8 0.7 fusion.2
  177.8 1.6 collective-permute-done.4.refs_3_
  179.4 0.8 place.1
  (46 shorter events, 4.5 us)
Async XLA Ops:
  7.2 125.4 %all-gather.2.cloned.1.call-start = ((), (), s32[]{:S(2)}) async-start(), calls=%async_computation.5 | async-start | bytes 33816576 | tf_op jit(solution)/shard_map/all_gather | solution.py:417
  7.2 0.9 copy-start
  8.1 0.8 copy-start.1
  8.9 13.9 %copy-start.3 = (bf16[64,16,256]{2,1,0:T(8,128)(2,1)S(1)}, bf16[64,16,256]{2,1,0:T(8,128)(2,1)}, u32[]{:S(2)}) copy-start(bf16[64,16,256]{2,1,0:T(8,128)(2,1)} %param.14) | copy-start | bytes 1572868
  11.3 26.3 %all-to-all-start = ((bf16[128,16,128]{2,1,0:T(8,128)(2,1)}), bf16[128,16,128]{2,1,0:T(8,128)(2,1)S(1)}, u32[]{:S(2)}, u32[]{:S(2)}) async-start(bf16[128,16,128]{2,1,0:T(8,128)(2,1)} %broadcast_in_dim.20), calls=%async_computation | async-start | bytes 1048576 | tf_op jit(solution)/shard_map/all_to_all | solution.py:422
  25.7 15.5 %copy-start.10 = (s32[8]{0:T(128)S(1)}, s32[8]{0:T(128)}, u32[]{:S(2)}) copy-start(s32[8]{0:T(128)} %param.11) | copy-start | bytes 100
  25.7 15.5 %copy-start.9 = (s32[8]{0:T(128)S(1)}, s32[8]{0:T(128)}, u32[]{:S(2)}) copy-start(s32[8]{0:T(128)} %param.10) | copy-start | bytes 100
  25.7 15.6 %copy-start.7 = (f32[2,2,256]{2,1,0:T(2,128)S(1)}, f32[2,2,256]{2,1,0:T(2,128)}, u32[]{:S(2)}) copy-start(f32[2,2,256]{2,1,0:T(2,128)} %param.15) | copy-start | bytes 12292
  25.7 32.5 %copy-start.6 = (f32[2048]{0:T(1024)S(1)}, f32[2048]{0:T(1024)}, u32[]{:S(2)}) copy-start(f32[2048]{0:T(1024)} %param.13) | copy-start | bytes 24580
  37.6 21.6 %copy-start.4 = (bf16[128,16,128]{2,1,0:T(8,128)(2,1)}, bf16[128,16,128]{2,1,0:T(8,128)(2,1)S(1)}, u32[]{:S(2)}) copy-start(bf16[128,16,128]{2,1,0:T(8,128)(2,1)S(1)} %all-to-all-done) | copy-start | bytes 1572868
  37.6 12.5 %all-to-all-start.1 = ((bf16[16,64,256]{2,1,0:T(8,128)(2,1)}), bf16[16,64,256]{2,1,0:T(8,128)(2,1)S(1)}, u32[]{:S(2)}, u32[]{:S(2)}) async-start(bf16[16,64,256]{2,1,0:T(8,128)(2,1)} %reshape.35), calls=%async_computation.1 | async-start | bytes 1048576 | tf_op jit(solution)/shard_map/all_to_all | solution.py:435
  50.1 9.1 %copy-start.5 = (bf16[16,64,256]{2,1,0:T(8,128)(2,1)}, bf16[16,64,256]{2,1,0:T(8,128)(2,1)S(1)}, u32[]{:S(2)}) copy-start(bf16[16,64,256]{2,1,0:T(8,128)(2,1)S(1)} %all-to-all-done.1.own_ref) | copy-start | bytes 1572868
  50.8 25.5 %all-to-all-start.3 = ((f32[4,8,256]{2,1,0:T(8,128)}), f32[4,8,256]{2,1,0:T(8,128)S(1)}, u32[]{:S(2)}, u32[]{:S(2)}) async-start(f32[4,8,256]{2,1,0:T(8,128)} %broadcast_in_dim.22), calls=%async_computation.3 | async-start | bytes 65536 | tf_op jit(solution)/shard_map/all_to_all | solution.py:447
  54.5 4.6 %collective-permute-start = (bf16[16,64,256]{2,1,0:T(8,128)(2,1)S(1)}, bf16[16,64,256]{2,1,0:T(8,128)(2,1)S(1)}, u32[]{:S(2)}, u32[]{:S(2)}) collective-permute-start(bf16[16,64,256]{2,1,0:T(8,128)(2,1)S(1)} %all-to-all-done.1.own_ref), channel_id=1, source_target_pairs={{0,1},{1,0},{2,3},{3,2},{4,5},{5,4},{6,7},{7,6},{8,9},{9,8},{10,11... | collective-permute-start | bytes 1572872 | tf_op jit(solution)/shard_map/ppermute | solution.py:436
  59.2 0.8 copy-start.8
  76.3 29.4 %all-to-all-start.2 = ((bf16[64,48,128]{2,1,0:T(8,128)(2,1)}), bf16[64,48,128]{2,1,0:T(8,128)(2,1)S(1)}, u32[]{:S(2)}, u32[]{:S(2)}) async-start(bf16[64,48,128]{2,1,0:T(8,128)(2,1)} %front.1), calls=%async_computation.2 | async-start | bytes 1572864 | tf_op jit(solution)/shard_map/all_to_all | solution.py:443
  105.6 0.9 copy-start.2
  153.2 1.6 collective-permute-start.5
  156.6 20.1 %all-to-all-start.4 = ((f32[64,8,8]{2,1,0:T(8,128)}), f32[64,8,8]{2,1,0:T(8,128)S(1)}, u32[]{:S(2)}, u32[]{:S(2)}) async-start(f32[64,8,8]{2,1,0:T(8,128)} %pad_maximum_fusion), calls=%async_computation.4 | async-start | bytes 524288 | tf_op jit(solution)/shard_map/all_to_all | solution.py:457
  164.7 12.8 %collective-permute-start.1 = (bf16[4,64,256]{2,1,0:T(8,128)(2,1)}, bf16[4,64,256]{2,1,0:T(8,128)(2,1)S(1)}, u32[]{:S(2)}, u32[]{:S(2)}) collective-permute-start(bf16[4,64,256]{2,1,0:T(8,128)(2,1)} %get-tuple-element.12), channel_id=1, source_target_pairs={{0,0},{1,32},{32,64},{33,96},{64,1},{65,33},{96,65},{97,97},{2,2},... | collective-permute-start | bytes 393224 | tf_op jit(solution)/shard_map/ppermute | solution.py:466
  168.3 9.1 %collective-permute-start.2 = (bf16[4,64,256]{2,1,0:T(8,128)(2,1)}, bf16[4,64,256]{2,1,0:T(8,128)(2,1)S(1)}, u32[]{:S(2)}, u32[]{:S(2)}) collective-permute-start(bf16[4,64,256]{2,1,0:T(8,128)(2,1)} %get-tuple-element.13), channel_id=1, source_target_pairs={{0,32},{1,64},{32,96},{33,0},{64,33},{65,65},{96,97},{97,1},{2,34}... | collective-permute-start | bytes 393224 | tf_op jit(solution)/shard_map/ppermute | solution.py:466
  171.9 5.9 %collective-permute-start.3 = (bf16[4,64,256]{2,1,0:T(8,128)(2,1)}, bf16[4,64,256]{2,1,0:T(8,128)(2,1)S(1)}, u32[]{:S(2)}, u32[]{:S(2)}) collective-permute-start(bf16[4,64,256]{2,1,0:T(8,128)(2,1)} %get-tuple-element.14), channel_id=1, source_target_pairs={{0,64},{1,96},{32,0},{33,32},{64,65},{65,97},{96,1},{97,33},{2,66}... | collective-permute-start | bytes 393224 | tf_op jit(solution)/shard_map/ppermute | solution.py:466
  171.9 7.4 %collective-permute-start.4 = (bf16[4,64,256]{2,1,0:T(8,128)(2,1)}, bf16[4,64,256]{2,1,0:T(8,128)(2,1)S(1)}, u32[]{:S(2)}, u32[]{:S(2)}) collective-permute-start(bf16[4,64,256]{2,1,0:T(8,128)(2,1)} %get-tuple-element.15), channel_id=1, source_target_pairs={{0,96},{1,0},{32,32},{33,64},{64,97},{65,1},{96,33},{97,65},{2,98}... | collective-permute-start | bytes 393224 | tf_op jit(solution)/shard_map/ppermute | solution.py:466
Sparse Core Ops, SparseCore 0:
  11.0 121.5 all-gather.1

commit v3 on v2

--- a/solution.py
+++ b/solution.py
@@ -136,7 +136,7 @@
 ):
     phases, halves, groups, rows, lanes = x_ref.shape
     dec_refs = refs[:groups]
-    near_ref, far_ref, w_s, p_s, act_s, a1_s, x1_s, acc_s, b_s, t_s, o_s, w_sem, p_sem = refs[groups:]
+    energy_ref, w_s, p_s, act_s, a1_s, x1_s, acc_s, b_s, t_s, o_s, w_sem, p_sem = refs[groups:]
     taps = w_s.shape[2]
     width = halves * lanes
     channels = groups * width
@@ -148,8 +148,8 @@
     def fetch(unit):
         for g in range(groups):
             i = unit * groups + g
-            yield pltpu.make_async_copy(w_ref.at[g, :, unit * taps : (unit + 1) * taps], w_s.at[i], w_sem.at[i])
-        yield pltpu.make_async_copy(w_ref.at[:, :, units * taps + unit], p_s.at[unit], p_sem.at[unit])
+            yield pltpu.make_async_copy(w_ref.at[g, :, unit, 0:taps], w_s.at[i], w_sem.at[i])
+        yield pltpu.make_async_copy(w_ref.at[:, :, unit, taps], p_s.at[unit], p_sem.at[unit])
 
     for copy in list(fetch(0))[: groups // 2]:
         copy.start()
@@ -162,7 +162,7 @@
     slot = row & (slots - 1)
     limit = jnp.zeros((kept, lanes), jnp.int32)
     for k in range(slots):
-        limit = jnp.where(slot == k, info_ref[4 + k], limit)
+        limit = jnp.where(slot == k, info_ref[3 + k], limit)
     live = jnp.where(at < limit, 1.0, 0.0).astype(F32)
 
     for s in range(phases):
@@ -234,13 +234,10 @@
                         ]
                 t_s[...] = squares
                 sums = sum(t_s[f * slots : (f + 1) * slots, :] for f in range(frames))
-                share = near_ref.shape[2]
-                for j in range(0, lanes // share, 2):
-                    even = sums if j == 0 else pltpu.roll(sums, lanes - j * share, 1)
-                    odd = pltpu.roll(sums, lanes - (j + 1) * share, 1)
-                    chip = lax.div(g * (width // share) + h * (lanes // share) + j, 2)
-                    near_ref[chip] = jnp.where(info_ref[3] == 0, even, odd)[:, :share]
-                    far_ref[chip] = jnp.where(info_ref[3] == 0, odd, even)[:, :share]
+                share = energy_ref.shape[2]
+                for j in range(lanes // share):
+                    moved = sums if j == 0 else pltpu.roll(sums, lanes - j * share, 1)
+                    energy_ref[g * (width // share) + h * (lanes // share) + j] = moved[:, :share]
                 for k in range(slots):
                     dec_refs[order][k, :, inner] = o_s[k * frames * phases : (k + 1) * frames * phases, :].astype(BF)
 
@@ -256,22 +253,6 @@
 
 def cost(flops, moved):
     return pl.CostEstimate(flops=flops, bytes_accessed=moved, transcendentals=0)
-
-
-def run_pack(first, second):
-    n = first.shape[0]
-
-    def pack_kernel(first_ref, second_ref, out_ref):
-        out_ref[0:n] = first_ref[...]
-        out_ref[n:] = second_ref[...]
-
-    return pl.pallas_call(
-        pack_kernel,
-        out_shape=jax.ShapeDtypeStruct((n + second.shape[0], *first.shape[1:]), first.dtype),
-        compiler_params=pltpu.CompilerParams(vmem_limit_bytes=VMEM // 4),
-        cost_estimate=cost(0, 4 * (first.size + second.size)),
-        name="pack",
-    )(first, second)
 
 
 def run_front(info, lat, w_in, freq, own, other, slots, chips):
@@ -325,9 +306,8 @@
 
 def run_units(info, act, x, freq, weights, slots, devices):
     phases, halves, groups, rows, lanes = x.shape
-    _, shards, kinds, depth, width = weights.shape
-    units = freq.shape[0]
-    taps = kinds // units - 1
+    _, shards, units, kinds, depth, width = weights.shape
+    taps = kinds - 1
     kept = rows - 2 * EDGE * slots
     channels = groups * width
     m = phases * kept
@@ -342,10 +322,10 @@
             vmem,
             pl.BlockSpec(memory_space=pl.ANY),
         ],
-        out_specs=[vmem] * (groups + 2),
+        out_specs=[vmem] * (groups + 1),
         out_shape=[
             *[jax.ShapeDtypeStruct((slots, m // slots, width), BF)] * groups,
-            *[jax.ShapeDtypeStruct((devices // 2, slots, channels // devices), F32)] * 2,
+            jax.ShapeDtypeStruct((devices, slots, channels // devices), F32),
         ],
         scratch_shapes=[
             pltpu.VMEM((units * groups, shards, taps, depth, width), BF),
@@ -361,7 +341,7 @@
             pltpu.SemaphoreType.DMA((units,)),
         ],
         compiler_params=pltpu.CompilerParams(vmem_limit_bytes=VMEM),
-        cost_estimate=cost((phases * rows + m) * kinds * channels * channels, 2 * weights.size),
+        cost_estimate=cost(2 * (phases * rows + m) * kinds * channels * channels, 2 * weights.size),
         name="units",
     )(info, act, x, freq, weights)
 
@@ -412,10 +392,10 @@
     lanes = c1_local // halves
     first_slot = ic * slots
 
-    weights = run_pack(dilated_conv_weight.reshape(-1, *dilated_conv_weight.shape[2:]), pointwise_conv_weight)
-    kinds = weights.shape[0]
-    weights = lax.all_gather(weights, everyone, axis=0, tiled=True)
-    weights = weights.reshape(ny, nx * nz * nc, kinds, *weights.shape[1:])
+    weights = jnp.concatenate([dilated_conv_weight, pointwise_conv_weight[:, None]], axis=1)
+    shape = weights.shape
+    weights = lax.all_gather(weights.reshape(-1, *shape[2:]), everyone, axis=0, tiled=True)
+    weights = weights.reshape(ny, nx * nz * nc, *shape)
 
     packed = latent.transpose(1, 0, 2).reshape(here_frames, here_clips * width_in)
     packed = jnp.broadcast_to(packed[None], (ny * nx * nz * nc,) + packed.shape)
@@ -440,6 +420,7 @@
     info = jnp.concatenate([info, my_dest, my_lengths]).astype(jnp.int32)
     packed = packed.reshape(ny, frames, here_clips * width_in)
     x = run_front(info, packed, w_in, freq_rows(snake_entry_frequency), own, other, slots, chips)
+    x, snake_unit_frequency = lax.optimization_barrier((x, snake_unit_frequency))
     x = lax.all_to_all(x, blocks, 0, 0, tiled=True)
     x = x.reshape(phases, halves, ny, x.shape[1], lanes)
 
@@ -449,12 +430,11 @@
 
     block = (ix * nz + iz) * ny + iy
     start = 2 * (iy % 2) + ic
-    info = jnp.concatenate([jnp.stack([block * own_frames, frames, start, ic]), my_lengths]).astype(jnp.int32)
+    info = jnp.concatenate([jnp.stack([block * own_frames, frames, start]), my_lengths]).astype(jnp.int32)
     act = run_activate(x, freq, slots, taps // 2)
-    *decoded, near, far = run_units(info, act, x, freq, weights, slots, ny * nx * nz * nc)
-
-    far = lax.ppermute(far, "c", [(i, nc - 1 - i) for i in range(nc)])
-    squares = lax.all_to_all(jnp.concatenate([near, far], axis=1), ("y", "x", "z"), 0, 0, tiled=True)
+    *decoded, squares = run_units(info, act, x, freq, weights, slots, ny * nx * nz * nc)
+
+    squares = lax.all_to_all(squares, everyone, 0, 0, tiled=True)
 
     pieces = []
     for k, piece in enumerate(decoded):
@@ -466,8 +446,7 @@
         pieces.append(lax.ppermute(piece, ("y", "c"), pairs))
     decoded = run_place(iy[None].astype(jnp.int32), pieces)
 
-    squares = squares.sum(axis=0)
-    squares = jnp.where(ic == 0, squares, jnp.roll(squares, slots, axis=0))
+    squares = squares.reshape(chips, clips, -1).sum(axis=0)
     count = (phases * lengths[:, None]).astype(F32)
     energy = jnp.log(squares / count + 1e-06)
     return decoded, energy

time: 188 us -> 183 us (0.973)
  starting transfers between devices: 49.4 us -> 42.3 us
  blocking collectives: 0 us -> 7.02 us
  local copies, waits for them, and re-layouts: 11.6 us -> 8.61 us
    all_to_all x0 -> x1, blocking collectives: none -> 7.02 us  [body(): lax.all_to_all(jnp.broadcast_to(freq, (ny,) + freq.shape[1:]), 'y', 0, 0,...]
    all_to_all x2 -> x1, starting transfers between devices: 11.9 us -> 7.22 us  [body(): squares = lax.all_to_all(squares, everyone, 0, 0, tiled=True)]
    all_to_all x1, starting transfers between devices: 7.05 us -> 4.83 us  [body(): x = lax.all_to_all(x, blocks, 0, 0, tiled=True)]
  transfers between devices with their start and end apart: 12 -> 10, of which waited for: 8 -> 7; matrix products, arithmetic and copies ran while one was open for 5% -> 5% of each run, Pallas kernels for 10% -> 11%
where the time goes in v3:
time: 183 us
  waiting for transfers between devices  64.6 us (35%)
  starting transfers between devices  42.3 us (23%)
  Pallas kernels  41.4 us (23%)
  between operations  14.3 us (8%)
  local copies, waits for them, and re-layouts  8.61 us (5%)
  blocking collectives  7.02 us (4%)
  other arithmetic  4.44 us (2%)
    all_gather x1, waiting for transfers between devices, body(): lax.all_gather(weights.reshape(-1, *shape[2:]), everyone, axis=0, tiled=T...  22.2 us
    pallas_call x1, Pallas kernels, run_units(): pl.pallas_call(functools.partial(units_kernel, slots), in_specs=[pl.Block...  20.6 us
    all_to_all x1, waiting for transfers between devices, body(): x = lax.all_to_all(x, blocks, 0, 0, tiled=True)  20.6 us
    pallas_call x1, Pallas kernels, run_front(): pl.pallas_call(functools.partial(front_kernel, slots), grid=(rows // ROW_...  16.4 us
    ppermute x4, starting transfers between devices, body(): pieces.append(lax.ppermute(piece, ('y', 'c'), pairs))  11.7 us
    all_to_all x1, starting transfers between devices, body(): packed = lax.all_to_all(packed, everyone, 0, 0, tiled=True)  11.5 us
    all_to_all x1, waiting for transfers between devices, body(): packed = lax.all_to_all(packed, everyone, 0, 0, tiled=True)  10.2 us
    all_to_all x1, waiting for transfers between devices, body(): own = lax.all_to_all(up, ('x', 'z'), 0, 0, tiled=True)  8.8 us
  transfers between devices with their start and end apart: 10, of which 7 were waited for; matrix products, arithmetic and copies ran while one was open for 5% of the time, Pallas kernels for 11%

profile of v3, /device:TPU:1, one launch (start us, length us, event | category | flops | bytes accessed | tf_op | source)
XLA Modules:
  0.0 182.6 jit_solution(8506463951674378729)
XLA Ops:
  7.2 1.8 pad_maximum_fusion
  9.0 0.7 copy.18
  9.8 0.9 broadcast_in_dim.23
  10.7 11.5 %all-to-all-start = ((bf16[128,16,128]{2,1,0:T(8,128)(2,1)}), bf16[128,16,128]{2,1,0:T(8,128)(2,1)S(1)}, u32[]{:S(2)}, u32[]{:S(2)}) async-start(bf16[128,16,128]{2,1,0:T(8,128)(2,1)} %broadcast_in_dim.23), calls=%async_computation | async-start | bytes 1048576 | tf_op jit(solution)/shard_map/all_to_all | solution.py:402
  22.2 1.1 fusion
  23.3 1.6 stack.37
  25.5 1.1 reshape.38
  26.6 10.2 %all-to-all-done = bf16[128,16,128]{2,1,0:T(8,128)(2,1)S(1)} async-done(((bf16[128,16,128]{2,1,0:T(8,128)(2,1)}), bf16[128,16,128]{2,1,0:T(8,128)(2,1)S(1)}, u32[]{:S(2)}, u32[]{:S(2)}) %all-to-all-start) | async-done | bytes 524320 | tf_op jit(solution)/shard_map/all_to_all | solution.py:402
  36.8 3.6 %all-to-all-start.1 = ((bf16[16,64,256]{2,1,0:T(8,128)(2,1)}), bf16[16,64,256]{2,1,0:T(8,128)(2,1)S(1)}, u32[]{:S(2)}, u32[]{:S(2)}) async-start(bf16[16,64,256]{2,1,0:T(8,128)(2,1)} %reshape.38), calls=%async_computation.1 | async-start | bytes 1048576 | tf_op jit(solution)/shard_map/all_to_all | solution.py:415
  40.6 8.8 %all-to-all-done.1.own_ref = bf16[16,64,256]{2,1,0:T(8,128)(2,1)S(1)} async-done(((bf16[16,64,256]{2,1,0:T(8,128)(2,1)}), bf16[16,64,256]{2,1,0:T(8,128)(2,1)S(1)}, u32[]{:S(2)}, u32[]{:S(2)}) %all-to-all-start.1) | async-done | bytes 524320 | tf_op jit(solution)/shard_map/all_to_all | solution.py:415
  49.4 3.5 %collective-permute-start = (bf16[16,64,256]{2,1,0:T(8,128)(2,1)S(1)}, bf16[16,64,256]{2,1,0:T(8,128)(2,1)S(1)}, u32[]{:S(2)}, u32[]{:S(2)}) collective-permute-start(bf16[16,64,256]{2,1,0:T(8,128)(2,1)S(1)} %all-to-all-done.1.own_ref), channel_id=1, source_target_pairs={{0,1},{1,0},{2,3},{3,2},{4,5},{5,4},{6,7},{7,6},{8,9},{9,8},{10,11... | collective-permute-start | bytes 1572872 | tf_op jit(solution)/shard_map/ppermute | solution.py:416
  52.9 0.7 pad_add_fusion.1.info_ref
  53.5 0.6 pad_maximum_fusion.1.freq_ref
  54.4 0.8 copy-done.6
  55.2 16.4 %front.1 = bf16[64,48,128]{2,1,0:T(8,128)(2,1)} custom-call(s32[10]{0:T(128)} %pad_add_fusion.1.info_ref, bf16[4,512,128]{2,1,0:T(8,128)(2,1)} %bitcast.36, bf16[448,2048]{1,0:T(8,128)(2,1)} %bitcast.43, f32[2,2048]{1,0:T(2,128)} %pad_maximum_fusion.1.freq_ref, bf16[16,64,256]{2,1,0:T(8,128)(2,1)} %copy-done.3, bf16[16,64,256]{2,1,0:T(8,128)(2,1)} %copy-done.6), custom_call_target="tpu_custom_call" | custom-call | flops 5905580032 | bytes 1835008 | tf_op jit(solution)/shard_map/front/pallas_call | solution.py:268
  71.6 7.0 %all_to_all.25 = f32[4,8,256]{2,1,0:T(8,128)S(1)} all-to-all(f32[4,8,256]{2,1,0:T(8,128)S(1)} %broadcast_in_dim.25), channel_id=1, replica_groups=mesh['y'=4,'x'=4,'z'=4,'c'=2] {'y'}, dimensions={0} | all-to-all | bytes 65536 | tf_op jit(solution)/shard_map/all_to_all | solution.py:428
  78.6 4.8 %all-to-all-start.2 = ((bf16[64,48,128]{2,1,0:T(8,128)(2,1)}), bf16[64,48,128]{2,1,0:T(8,128)(2,1)S(1)}, u32[]{:S(2)}, u32[]{:S(2)}) async-start(bf16[64,48,128]{2,1,0:T(8,128)(2,1)} %front.1), calls=%async_computation.2 | async-start | bytes 1572864 | tf_op jit(solution)/shard_map/all_to_all | solution.py:424
  83.5 0.6 pad_add_fusion.info_ref
  84.1 0.6 reshape.42.freq_ref
  84.8 20.6 %all-to-all-done.2 = bf16[64,48,128]{2,1,0:T(8,128)(2,1)S(1)} async-done(((bf16[64,48,128]{2,1,0:T(8,128)(2,1)}), bf16[64,48,128]{2,1,0:T(8,128)(2,1)S(1)}, u32[]{:S(2)}, u32[]{:S(2)}) %all-to-all-start.2) | async-done | bytes 786464 | tf_op jit(solution)/shard_map/all_to_all | solution.py:424
  105.4 0.9 copy-done
  106.3 3.5 %activate.1.a0_ref = bf16[14,48,1024]{2,1,0:T(8,128)(2,1)} custom-call(bf16[8,2,4,48,128]{4,3,2,1,0:T(8,128)(2,1)} %bitcast.30, f32[2,4,1024]{2,1,0:T(4,128)} %reshape.42.freq_ref), custom_call_target="tpu_custom_call" | custom-call | flops 7864320 | bytes 2359296 | tf_op jit(solution)/shard_map/activate/pallas_call | solution.py:297
  109.8 22.2 %all-gather.2.cloned.1.call-done = bf16[2048,32,256]{2,1,0:T(8,128)(2,1)} async-done(((bf16[16,32,256]{2,1,0:T(8,128)(2,1)}), bf16[2048,32,256]{2,1,0:T(8,128)(2,1)}) %all-gather.2.cloned.1.call-update) | async-done | bytes 33554448 | tf_op jit(solution)/shard_map/all_gather | solution.py:397
  132.1 20.6 %units.1 = (bf16[4,64,256]{2,1,0:T(8,128)(2,1)}, bf16[4,64,256]{2,1,0:T(8,128)(2,1)}, bf16[4,64,256]{2,1,0:T(8,128)(2,1)}, bf16[4,64,256]{2,1,0:T(8,128)(2,1)}, f32[128,4,8]{2,1,0:T(4,128)}) custom-call(s32[7]{0:T(128)} %pad_add_fusion.info_ref, bf16[14,48,1024]{2,1,0:T(8,128)(2,1)} %activate.1.a0_ref, bf16[8,2,4,48,128]{4,3,2,1,0:T(8,128)(2,1)} %bitcast.31, ...), custom_call_target="tpu_custom_call" | custom-call | flops 10737418240 | bytes 33554432 | tf_op jit(solution)/shard_map/units/pallas_call | solution.py:316
  152.7 7.2 %all-to-all-start.4 = ((f32[128,4,8]{2,1,0:T(4,128)}), f32[128,4,8]{2,1,0:T(4,128)S(1)}, u32[]{:S(2)}, u32[]{:S(2)}) async-start(f32[128,4,8]{2,1,0:T(4,128)} %get-tuple-element.19), calls=%async_computation.4 | async-start | bytes 524288 | tf_op jit(solution)/shard_map/all_to_all | solution.py:437
  160.0 3.5 %collective-permute-start.1 = (bf16[4,64,256]{2,1,0:T(8,128)(2,1)}, bf16[4,64,256]{2,1,0:T(8,128)(2,1)S(1)}, u32[]{:S(2)}, u32[]{:S(2)}) collective-permute-start(bf16[4,64,256]{2,1,0:T(8,128)(2,1)} %get-tuple-element.15), channel_id=1, source_target_pairs={{0,0},{1,32},{32,64},{33,96},{64,1},{65,33},{96,65},{97,97},{2,2},... | collective-permute-start | bytes 393224 | tf_op jit(solution)/shard_map/ppermute | solution.py:446
  163.5 3.5 %collective-permute-start.2 = (bf16[4,64,256]{2,1,0:T(8,128)(2,1)}, bf16[4,64,256]{2,1,0:T(8,128)(2,1)S(1)}, u32[]{:S(2)}, u32[]{:S(2)}) collective-permute-start(bf16[4,64,256]{2,1,0:T(8,128)(2,1)} %get-tuple-element.16), channel_id=1, source_target_pairs={{0,32},{1,64},{32,96},{33,0},{64,33},{65,65},{96,97},{97,1},{2,34}... | collective-permute-start | bytes 393224 | tf_op jit(solution)/shard_map/ppermute | solution.py:446
  167.3 4.4 %collective-permute-start.4 = (bf16[4,64,256]{2,1,0:T(8,128)(2,1)}, bf16[4,64,256]{2,1,0:T(8,128)(2,1)S(1)}, u32[]{:S(2)}, u32[]{:S(2)}) collective-permute-start(bf16[4,64,256]{2,1,0:T(8,128)(2,1)} %get-tuple-element.18), channel_id=1, source_target_pairs={{0,96},{1,0},{32,32},{33,64},{64,97},{65,1},{96,33},{97,65},{2,98}... | collective-permute-start | bytes 393224 | tf_op jit(solution)/shard_map/ppermute | solution.py:446
  171.8 0.7 add_log_fusion
  172.5 0.5 collective-permute-done.3.refs_2_
  172.9 2.0 %collective-permute-done.4.refs_3_ = bf16[4,64,256]{2,1,0:T(8,128)(2,1)S(1)} collective-permute-done((bf16[4,64,256]{2,1,0:T(8,128)(2,1)}, bf16[4,64,256]{2,1,0:T(8,128)(2,1)S(1)}, u32[]{:S(2)}, u32[]{:S(2)}) %collective-permute-start.4) | collective-permute-done | bytes 131104 | tf_op jit(solution)/shard_map/ppermute | solution.py:446
  174.9 0.8 place.1
  (37 shorter events, 1.5 us)
Async XLA Ops:
  7.2 15.0 %copy-start.1 = (bf16[64,16,256]{2,1,0:T(8,128)(2,1)S(1)}, bf16[64,16,256]{2,1,0:T(8,128)(2,1)}, u32[]{:S(2)}) copy-start(bf16[64,16,256]{2,1,0:T(8,128)(2,1)} %param.14) | copy-start | bytes 1572868
  7.2 124.9 %all-gather.2.cloned.1.call-start = ((), (), s32[]{:S(2)}) async-start(), calls=%async_computation.5 | async-start | bytes 33816576 | tf_op jit(solution)/shard_map/all_gather | solution.py:397
  10.7 26.2 %all-to-all-start = ((bf16[128,16,128]{2,1,0:T(8,128)(2,1)}), bf16[128,16,128]{2,1,0:T(8,128)(2,1)S(1)}, u32[]{:S(2)}, u32[]{:S(2)}) async-start(bf16[128,16,128]{2,1,0:T(8,128)(2,1)} %broadcast_in_dim.23), calls=%async_computation | async-start | bytes 1048576 | tf_op jit(solution)/shard_map/all_to_all | solution.py:402
  25.1 15.4 %copy-start.8 = (s32[8]{0:T(128)S(1)}, s32[8]{0:T(128)}, u32[]{:S(2)}) copy-start(s32[8]{0:T(128)} %param.11) | copy-start | bytes 100
  25.1 15.4 %copy-start.7 = (s32[8]{0:T(128)S(1)}, s32[8]{0:T(128)}, u32[]{:S(2)}) copy-start(s32[8]{0:T(128)} %param.10) | copy-start | bytes 100
  25.1 28.4 %copy-start.4 = (f32[2048]{0:T(1024)S(1)}, f32[2048]{0:T(1024)}, u32[]{:S(2)}) copy-start(f32[2048]{0:T(1024)} %param.13) | copy-start | bytes 24580
  36.8 17.6 %copy-start.2 = (bf16[128,16,128]{2,1,0:T(8,128)(2,1)}, bf16[128,16,128]{2,1,0:T(8,128)(2,1)S(1)}, u32[]{:S(2)}) copy-start(bf16[128,16,128]{2,1,0:T(8,128)(2,1)S(1)} %all-to-all-done) | copy-start | bytes 1572868
  36.8 12.6 %all-to-all-start.1 = ((bf16[16,64,256]{2,1,0:T(8,128)(2,1)}), bf16[16,64,256]{2,1,0:T(8,128)(2,1)S(1)}, u32[]{:S(2)}, u32[]{:S(2)}) async-start(bf16[16,64,256]{2,1,0:T(8,128)(2,1)} %reshape.38), calls=%async_computation.1 | async-start | bytes 1048576 | tf_op jit(solution)/shard_map/all_to_all | solution.py:415
  49.4 5.0 %copy-start.3 = (bf16[16,64,256]{2,1,0:T(8,128)(2,1)}, bf16[16,64,256]{2,1,0:T(8,128)(2,1)S(1)}, u32[]{:S(2)}) copy-start(bf16[16,64,256]{2,1,0:T(8,128)(2,1)S(1)} %all-to-all-done.1.own_ref) | copy-start | bytes 1572868
  49.4 5.0 %collective-permute-start = (bf16[16,64,256]{2,1,0:T(8,128)(2,1)S(1)}, bf16[16,64,256]{2,1,0:T(8,128)(2,1)S(1)}, u32[]{:S(2)}, u32[]{:S(2)}) collective-permute-start(bf16[16,64,256]{2,1,0:T(8,128)(2,1)S(1)} %all-to-all-done.1.own_ref), channel_id=1, source_target_pairs={{0,1},{1,0},{2,3},{3,2},{4,5},{5,4},{6,7},{7,6},{8,9},{9,8},{10,11... | collective-permute-start | bytes 1572872 | tf_op jit(solution)/shard_map/ppermute | solution.py:416
  54.4 0.8 copy-start.6
  55.2 16.4 %copy-start.5 = (f32[2,2,256]{2,1,0:T(2,128)S(1)}, f32[2,2,256]{2,1,0:T(2,128)}, u32[]{:S(2)}) copy-start(f32[2,2,256]{2,1,0:T(2,128)} %param.15) | copy-start | bytes 12292
  78.6 26.7 %all-to-all-start.2 = ((bf16[64,48,128]{2,1,0:T(8,128)(2,1)}), bf16[64,48,128]{2,1,0:T(8,128)(2,1)S(1)}, u32[]{:S(2)}, u32[]{:S(2)}) async-start(bf16[64,48,128]{2,1,0:T(8,128)(2,1)} %front.1), calls=%async_computation.2 | async-start | bytes 1572864 | tf_op jit(solution)/shard_map/all_to_all | solution.py:424
  105.4 0.9 copy-start
  152.7 19.0 %all-to-all-start.4 = ((f32[128,4,8]{2,1,0:T(4,128)}), f32[128,4,8]{2,1,0:T(4,128)S(1)}, u32[]{:S(2)}, u32[]{:S(2)}) async-start(f32[128,4,8]{2,1,0:T(4,128)} %get-tuple-element.19), calls=%async_computation.4 | async-start | bytes 524288 | tf_op jit(solution)/shard_map/all_to_all | solution.py:437
  160.0 12.5 %collective-permute-start.1 = (bf16[4,64,256]{2,1,0:T(8,128)(2,1)}, bf16[4,64,256]{2,1,0:T(8,128)(2,1)S(1)}, u32[]{:S(2)}, u32[]{:S(2)}) collective-permute-start(bf16[4,64,256]{2,1,0:T(8,128)(2,1)} %get-tuple-element.15), channel_id=1, source_target_pairs={{0,0},{1,32},{32,64},{33,96},{64,1},{65,33},{96,65},{97,97},{2,2},... | collective-permute-start | bytes 393224 | tf_op jit(solution)/shard_map/ppermute | solution.py:446
  163.5 9.0 %collective-permute-start.2 = (bf16[4,64,256]{2,1,0:T(8,128)(2,1)}, bf16[4,64,256]{2,1,0:T(8,128)(2,1)S(1)}, u32[]{:S(2)}, u32[]{:S(2)}) collective-permute-start(bf16[4,64,256]{2,1,0:T(8,128)(2,1)} %get-tuple-element.16), channel_id=1, source_target_pairs={{0,32},{1,64},{32,96},{33,0},{64,33},{65,65},{96,97},{97,1},{2,34}... | collective-permute-start | bytes 393224 | tf_op jit(solution)/shard_map/ppermute | solution.py:446
  167.0 5.9 %collective-permute-start.3 = (bf16[4,64,256]{2,1,0:T(8,128)(2,1)}, bf16[4,64,256]{2,1,0:T(8,128)(2,1)S(1)}, u32[]{:S(2)}, u32[]{:S(2)}) collective-permute-start(bf16[4,64,256]{2,1,0:T(8,128)(2,1)} %get-tuple-element.17), channel_id=1, source_target_pairs={{0,64},{1,96},{32,0},{33,32},{64,65},{65,97},{96,1},{97,33},{2,66}... | collective-permute-start | bytes 393224 | tf_op jit(solution)/shard_map/ppermute | solution.py:446
  167.3 7.6 %collective-permute-start.4 = (bf16[4,64,256]{2,1,0:T(8,128)(2,1)}, bf16[4,64,256]{2,1,0:T(8,128)(2,1)S(1)}, u32[]{:S(2)}, u32[]{:S(2)}) collective-permute-start(bf16[4,64,256]{2,1,0:T(8,128)(2,1)} %get-tuple-element.18), channel_id=1, source_target_pairs={{0,96},{1,0},{32,32},{33,64},{64,97},{65,1},{96,33},{97,65},{2,98}... | collective-permute-start | bytes 393224 | tf_op jit(solution)/shard_map/ppermute | solution.py:446
Sparse Core Ops, SparseCore 0:
  11.0 121.0 all-gather.1

commit v4 on v3

--- a/solution.py
+++ b/solution.py
@@ -420,8 +420,8 @@
     info = jnp.concatenate([info, my_dest, my_lengths]).astype(jnp.int32)
     packed = packed.reshape(ny, frames, here_clips * width_in)
     x = run_front(info, packed, w_in, freq_rows(snake_entry_frequency), own, other, slots, chips)
+    x = lax.all_to_all(x, blocks, 0, 0, tiled=True)
     x, snake_unit_frequency = lax.optimization_barrier((x, snake_unit_frequency))
-    x = lax.all_to_all(x, blocks, 0, 0, tiled=True)
     x = x.reshape(phases, halves, ny, x.shape[1], lanes)
 
     freq = freq_rows(snake_unit_frequency).reshape(1, -1, c1_local)

time: 183 us -> 183 us (level)
  blocking collectives: 7.02 us -> 0 us
  starting transfers between devices: 42.3 us -> 46.2 us
  waiting for transfers between devices: 64.6 us -> 68.1 us
    all_to_all x1 -> x0, blocking collectives: 7.02 us -> none  [body(): lax.all_to_all(jnp.broadcast_to(freq, (ny,) + freq.shape[1:]), 'y', 0, 0,...]
    all_to_all x0 -> x1, waiting for transfers between devices: none -> 4.01 us  [body(): lax.all_to_all(jnp.broadcast_to(freq, (ny,) + freq.shape[1:]), 'y', 0, 0,...]
    all_to_all x0 -> x1, starting transfers between devices: none -> 3.67 us  [body(): lax.all_to_all(jnp.broadcast_to(freq, (ny,) + freq.shape[1:]), 'y', 0, 0,...]
    all_gather x1, waiting for transfers between devices: 22.2 us -> 19.9 us  [body(): lax.all_gather(weights.reshape(-1, *shape[2:]), everyone, axis=0, tiled=T...]
  transfers between devices with their start and end apart: 10 -> 11, of which waited for: 7 -> 8; matrix products, arithmetic and copies ran while one was open for 5% -> 6% of each run, Pallas kernels for 11% -> 11%
where the time goes in v4:
time: 183 us
  waiting for transfers between devices  68.1 us (37%)
  starting transfers between devices  46.2 us (25%)
  Pallas kernels  41.1 us (22%)
  between operations  14.3 us (8%)
  local copies, waits for them, and re-layouts  8.41 us (5%)
  other arithmetic  4.45 us (2%)
    all_to_all x1, waiting for transfers between devices, body(): x = lax.all_to_all(x, blocks, 0, 0, tiled=True)  22.4 us
    pallas_call x1, Pallas kernels, run_units(): pl.pallas_call(functools.partial(units_kernel, slots), in_specs=[pl.Block...  20.6 us
    all_gather x1, waiting for transfers between devices, body(): lax.all_gather(weights.reshape(-1, *shape[2:]), everyone, axis=0, tiled=T...  19.9 us
    pallas_call x1, Pallas kernels, run_front(): pl.pallas_call(functools.partial(front_kernel, slots), grid=(rows // ROW_...  16.4 us
    ppermute x4, starting transfers between devices, body(): pieces.append(lax.ppermute(piece, ('y', 'c'), pairs))  11.7 us
    all_to_all x1, starting transfers between devices, body(): packed = lax.all_to_all(packed, everyone, 0, 0, tiled=True)  11.5 us
    all_to_all x1, waiting for transfers between devices, body(): packed = lax.all_to_all(packed, everyone, 0, 0, tiled=True)  10.2 us
    all_to_all x1, waiting for transfers between devices, body(): own = lax.all_to_all(up, ('x', 'z'), 0, 0, tiled=True)  8.8 us
  transfers between devices with their start and end apart: 11, of which 8 were waited for; matrix products, arithmetic and copies ran while one was open for 6% of the time, Pallas kernels for 11%

profile of v4, /device:TPU:1, one launch (start us, length us, event | category | flops | bytes accessed | tf_op | source)
XLA Modules:
  0.0 182.6 jit_solution(6379147191301890493)
XLA Ops:
  7.2 1.7 pad_maximum_fusion
  9.0 0.7 copy.18
  9.8 0.9 broadcast_in_dim.23
  10.6 11.5 %all-to-all-start = ((bf16[128,16,128]{2,1,0:T(8,128)(2,1)}), bf16[128,16,128]{2,1,0:T(8,128)(2,1)S(1)}, u32[]{:S(2)}, u32[]{:S(2)}) async-start(bf16[128,16,128]{2,1,0:T(8,128)(2,1)} %broadcast_in_dim.23), calls=%async_computation | async-start | bytes 1048576 | tf_op jit(solution)/shard_map/all_to_all | solution.py:402
  22.2 1.1 fusion
  23.3 1.6 stack.37
  25.5 1.1 reshape.38
  26.6 10.2 %all-to-all-done = bf16[128,16,128]{2,1,0:T(8,128)(2,1)S(1)} async-done(((bf16[128,16,128]{2,1,0:T(8,128)(2,1)}), bf16[128,16,128]{2,1,0:T(8,128)(2,1)S(1)}, u32[]{:S(2)}, u32[]{:S(2)}) %all-to-all-start) | async-done | bytes 524320 | tf_op jit(solution)/shard_map/all_to_all | solution.py:402
  36.8 3.6 %all-to-all-start.1 = ((bf16[16,64,256]{2,1,0:T(8,128)(2,1)}), bf16[16,64,256]{2,1,0:T(8,128)(2,1)S(1)}, u32[]{:S(2)}, u32[]{:S(2)}) async-start(bf16[16,64,256]{2,1,0:T(8,128)(2,1)} %reshape.38), calls=%async_computation.1 | async-start | bytes 1048576 | tf_op jit(solution)/shard_map/all_to_all | solution.py:415
  40.6 8.8 %all-to-all-done.1.own_ref = bf16[16,64,256]{2,1,0:T(8,128)(2,1)S(1)} async-done(((bf16[16,64,256]{2,1,0:T(8,128)(2,1)}), bf16[16,64,256]{2,1,0:T(8,128)(2,1)S(1)}, u32[]{:S(2)}, u32[]{:S(2)}) %all-to-all-start.1) | async-done | bytes 524320 | tf_op jit(solution)/shard_map/all_to_all | solution.py:415
  49.4 3.5 %collective-permute-start = (bf16[16,64,256]{2,1,0:T(8,128)(2,1)S(1)}, bf16[16,64,256]{2,1,0:T(8,128)(2,1)S(1)}, u32[]{:S(2)}, u32[]{:S(2)}) collective-permute-start(bf16[16,64,256]{2,1,0:T(8,128)(2,1)S(1)} %all-to-all-done.1.own_ref), channel_id=1, source_target_pairs={{0,1},{1,0},{2,3},{3,2},{4,5},{5,4},{6,7},{7,6},{8,9},{9,8},{10,11... | collective-permute-start | bytes 1572872 | tf_op jit(solution)/shard_map/ppermute | solution.py:416
  52.8 0.7 pad_add_fusion.1.info_ref
  53.5 0.6 pad_maximum_fusion.1.freq_ref
  54.4 0.8 copy-done.6
  55.2 16.4 %front.1 = bf16[64,48,128]{2,1,0:T(8,128)(2,1)} custom-call(s32[10]{0:T(128)} %pad_add_fusion.1.info_ref, bf16[4,512,128]{2,1,0:T(8,128)(2,1)} %bitcast.36, bf16[448,2048]{1,0:T(8,128)(2,1)} %bitcast.43, f32[2,2048]{1,0:T(2,128)} %pad_maximum_fusion.1.freq_ref, bf16[16,64,256]{2,1,0:T(8,128)(2,1)} %copy-done.3, bf16[16,64,256]{2,1,0:T(8,128)(2,1)} %copy-done.6), custom_call_target="tpu_custom_call" | custom-call | flops 5905580032 | bytes 1835008 | tf_op jit(solution)/shard_map/front/pallas_call | solution.py:268
  71.5 5.0 %all-to-all-start.2 = ((bf16[64,48,128]{2,1,0:T(8,128)(2,1)}), bf16[64,48,128]{2,1,0:T(8,128)(2,1)S(1)}, u32[]{:S(2)}, u32[]{:S(2)}) async-start(bf16[64,48,128]{2,1,0:T(8,128)(2,1)} %front.1), calls=%async_computation.2 | async-start | bytes 1572864 | tf_op jit(solution)/shard_map/all_to_all | solution.py:423
  76.6 22.4 %all-to-all-done.2 = bf16[64,48,128]{2,1,0:T(8,128)(2,1)S(1)} async-done(((bf16[64,48,128]{2,1,0:T(8,128)(2,1)}), bf16[64,48,128]{2,1,0:T(8,128)(2,1)S(1)}, u32[]{:S(2)}, u32[]{:S(2)}) %all-to-all-start.2) | async-done | bytes 786464 | tf_op jit(solution)/shard_map/all_to_all | solution.py:423
  99.1 0.7 broadcast_in_dim.25
  99.8 3.7 %all-to-all-start.3 = ((f32[4,8,256]{2,1,0:T(8,128)}), f32[4,8,256]{2,1,0:T(8,128)S(1)}, u32[]{:S(2)}, u32[]{:S(2)}) async-start(f32[4,8,256]{2,1,0:T(8,128)} %broadcast_in_dim.25), calls=%async_computation.3 | async-start | bytes 65536 | tf_op jit(solution)/shard_map/all_to_all | solution.py:428
  103.5 0.7 pad_add_fusion.info_ref
  104.1 4.0 %all-to-all-done.3 = f32[4,8,256]{2,1,0:T(8,128)S(1)} async-done(((f32[4,8,256]{2,1,0:T(8,128)}), f32[4,8,256]{2,1,0:T(8,128)S(1)}, u32[]{:S(2)}, u32[]{:S(2)}) %all-to-all-start.3) | async-done | bytes 32800 | tf_op jit(solution)/shard_map/all_to_all | solution.py:428
  108.2 0.6 reshape.42.freq_ref
  108.8 3.3 %activate.1.a0_ref = bf16[14,48,1024]{2,1,0:T(8,128)(2,1)} custom-call(bf16[8,2,4,48,128]{4,3,2,1,0:T(8,128)(2,1)} %bitcast.30, f32[2,4,1024]{2,1,0:T(4,128)} %reshape.42.freq_ref), custom_call_target="tpu_custom_call" | custom-call | flops 7864320 | bytes 2359296 | tf_op jit(solution)/shard_map/activate/pallas_call | solution.py:297
  112.1 19.9 %all-gather.2.cloned.1.call-done = bf16[2048,32,256]{2,1,0:T(8,128)(2,1)} async-done(((bf16[16,32,256]{2,1,0:T(8,128)(2,1)}), bf16[2048,32,256]{2,1,0:T(8,128)(2,1)}) %all-gather.2.cloned.1.call-update) | async-done | bytes 33554448 | tf_op jit(solution)/shard_map/all_gather | solution.py:397
  132.1 20.6 %units.1 = (bf16[4,64,256]{2,1,0:T(8,128)(2,1)}, bf16[4,64,256]{2,1,0:T(8,128)(2,1)}, bf16[4,64,256]{2,1,0:T(8,128)(2,1)}, bf16[4,64,256]{2,1,0:T(8,128)(2,1)}, f32[128,4,8]{2,1,0:T(4,128)}) custom-call(s32[7]{0:T(128)} %pad_add_fusion.info_ref, bf16[14,48,1024]{2,1,0:T(8,128)(2,1)} %activate.1.a0_ref, bf16[8,2,4,48,128]{4,3,2,1,0:T(8,128)(2,1)} %bitcast.31, ...), custom_call_target="tpu_custom_call" | custom-call | flops 10737418240 | bytes 33554432 | tf_op jit(solution)/shard_map/units/pallas_call | solution.py:316
  152.7 7.2 %all-to-all-start.4 = ((f32[128,4,8]{2,1,0:T(4,128)}), f32[128,4,8]{2,1,0:T(4,128)S(1)}, u32[]{:S(2)}, u32[]{:S(2)}) async-start(f32[128,4,8]{2,1,0:T(4,128)} %get-tuple-element.19), calls=%async_computation.4 | async-start | bytes 524288 | tf_op jit(solution)/shard_map/all_to_all | solution.py:437
  160.0 3.5 %collective-permute-start.1 = (bf16[4,64,256]{2,1,0:T(8,128)(2,1)}, bf16[4,64,256]{2,1,0:T(8,128)(2,1)S(1)}, u32[]{:S(2)}, u32[]{:S(2)}) collective-permute-start(bf16[4,64,256]{2,1,0:T(8,128)(2,1)} %get-tuple-element.15), channel_id=1, source_target_pairs={{0,0},{1,32},{32,64},{33,96},{64,1},{65,33},{96,65},{97,97},{2,2},... | collective-permute-start | bytes 393224 | tf_op jit(solution)/shard_map/ppermute | solution.py:446
  163.5 3.5 %collective-permute-start.2 = (bf16[4,64,256]{2,1,0:T(8,128)(2,1)}, bf16[4,64,256]{2,1,0:T(8,128)(2,1)S(1)}, u32[]{:S(2)}, u32[]{:S(2)}) collective-permute-start(bf16[4,64,256]{2,1,0:T(8,128)(2,1)} %get-tuple-element.16), channel_id=1, source_target_pairs={{0,32},{1,64},{32,96},{33,0},{64,33},{65,65},{96,97},{97,1},{2,34}... | collective-permute-start | bytes 393224 | tf_op jit(solution)/shard_map/ppermute | solution.py:446
  167.3 4.4 %collective-permute-start.4 = (bf16[4,64,256]{2,1,0:T(8,128)(2,1)}, bf16[4,64,256]{2,1,0:T(8,128)(2,1)S(1)}, u32[]{:S(2)}, u32[]{:S(2)}) collective-permute-start(bf16[4,64,256]{2,1,0:T(8,128)(2,1)} %get-tuple-element.18), channel_id=1, source_target_pairs={{0,96},{1,0},{32,32},{33,64},{64,97},{65,1},{96,33},{97,65},{2,98}... | collective-permute-start | bytes 393224 | tf_op jit(solution)/shard_map/ppermute | solution.py:446
  171.8 0.7 add_log_fusion
  172.9 2.0 %collective-permute-done.4.refs_3_ = bf16[4,64,256]{2,1,0:T(8,128)(2,1)S(1)} collective-permute-done((bf16[4,64,256]{2,1,0:T(8,128)(2,1)}, bf16[4,64,256]{2,1,0:T(8,128)(2,1)S(1)}, u32[]{:S(2)}, u32[]{:S(2)}) %collective-permute-start.4) | collective-permute-done | bytes 131104 | tf_op jit(solution)/shard_map/ppermute | solution.py:446
  174.9 0.8 place.1
  (38 shorter events, 2.0 us)
Async XLA Ops:
  7.2 15.0 %copy-start.1 = (bf16[64,16,256]{2,1,0:T(8,128)(2,1)S(1)}, bf16[64,16,256]{2,1,0:T(8,128)(2,1)}, u32[]{:S(2)}) copy-start(bf16[64,16,256]{2,1,0:T(8,128)(2,1)} %param.14) | copy-start | bytes 1572868
  7.2 124.9 %all-gather.2.cloned.1.call-start = ((), (), s32[]{:S(2)}) async-start(), calls=%async_computation.5 | async-start | bytes 33816576 | tf_op jit(solution)/shard_map/all_gather | solution.py:397
  10.6 26.2 %all-to-all-start = ((bf16[128,16,128]{2,1,0:T(8,128)(2,1)}), bf16[128,16,128]{2,1,0:T(8,128)(2,1)S(1)}, u32[]{:S(2)}, u32[]{:S(2)}) async-start(bf16[128,16,128]{2,1,0:T(8,128)(2,1)} %broadcast_in_dim.23), calls=%async_computation | async-start | bytes 1048576 | tf_op jit(solution)/shard_map/all_to_all | solution.py:402
  25.0 15.4 %copy-start.8 = (s32[8]{0:T(128)S(1)}, s32[8]{0:T(128)}, u32[]{:S(2)}) copy-start(s32[8]{0:T(128)} %param.11) | copy-start | bytes 100
  25.1 15.4 %copy-start.7 = (s32[8]{0:T(128)S(1)}, s32[8]{0:T(128)}, u32[]{:S(2)}) copy-start(s32[8]{0:T(128)} %param.10) | copy-start | bytes 100
  25.1 28.4 %copy-start.4 = (f32[2048]{0:T(1024)S(1)}, f32[2048]{0:T(1024)}, u32[]{:S(2)}) copy-start(f32[2048]{0:T(1024)} %param.13) | copy-start | bytes 24580
  36.8 17.6 %copy-start.2 = (bf16[128,16,128]{2,1,0:T(8,128)(2,1)}, bf16[128,16,128]{2,1,0:T(8,128)(2,1)S(1)}, u32[]{:S(2)}) copy-start(bf16[128,16,128]{2,1,0:T(8,128)(2,1)S(1)} %all-to-all-done) | copy-start | bytes 1572868
  36.8 12.6 %all-to-all-start.1 = ((bf16[16,64,256]{2,1,0:T(8,128)(2,1)}), bf16[16,64,256]{2,1,0:T(8,128)(2,1)S(1)}, u32[]{:S(2)}, u32[]{:S(2)}) async-start(bf16[16,64,256]{2,1,0:T(8,128)(2,1)} %reshape.38), calls=%async_computation.1 | async-start | bytes 1048576 | tf_op jit(solution)/shard_map/all_to_all | solution.py:415
  49.4 5.0 %copy-start.3 = (bf16[16,64,256]{2,1,0:T(8,128)(2,1)}, bf16[16,64,256]{2,1,0:T(8,128)(2,1)S(1)}, u32[]{:S(2)}) copy-start(bf16[16,64,256]{2,1,0:T(8,128)(2,1)S(1)} %all-to-all-done.1.own_ref) | copy-start | bytes 1572868
  49.4 5.0 %collective-permute-start = (bf16[16,64,256]{2,1,0:T(8,128)(2,1)S(1)}, bf16[16,64,256]{2,1,0:T(8,128)(2,1)S(1)}, u32[]{:S(2)}, u32[]{:S(2)}) collective-permute-start(bf16[16,64,256]{2,1,0:T(8,128)(2,1)S(1)} %all-to-all-done.1.own_ref), channel_id=1, source_target_pairs={{0,1},{1,0},{2,3},{3,2},{4,5},{5,4},{6,7},{7,6},{8,9},{9,8},{10,11... | collective-permute-start | bytes 1572872 | tf_op jit(solution)/shard_map/ppermute | solution.py:416
  54.4 0.8 copy-start.6
  55.2 43.9 %copy-start.5 = (f32[2,2,256]{2,1,0:T(2,128)S(1)}, f32[2,2,256]{2,1,0:T(2,128)}, u32[]{:S(2)}) copy-start(f32[2,2,256]{2,1,0:T(2,128)} %param.15) | copy-start | bytes 12292
  71.5 27.5 %all-to-all-start.2 = ((bf16[64,48,128]{2,1,0:T(8,128)(2,1)}), bf16[64,48,128]{2,1,0:T(8,128)(2,1)S(1)}, u32[]{:S(2)}, u32[]{:S(2)}) async-start(bf16[64,48,128]{2,1,0:T(8,128)(2,1)} %front.1), calls=%async_computation.2 | async-start | bytes 1572864 | tf_op jit(solution)/shard_map/all_to_all | solution.py:423
  99.1 9.8 %copy-start = (bf16[64,48,128]{2,1,0:T(8,128)(2,1)}, bf16[64,48,128]{2,1,0:T(8,128)(2,1)S(1)}, u32[]{:S(2)}) copy-start(bf16[64,48,128]{2,1,0:T(8,128)(2,1)S(1)} %all-to-all-done.2) | copy-start | bytes 2359300
  99.8 8.3 %all-to-all-start.3 = ((f32[4,8,256]{2,1,0:T(8,128)}), f32[4,8,256]{2,1,0:T(8,128)S(1)}, u32[]{:S(2)}, u32[]{:S(2)}) async-start(f32[4,8,256]{2,1,0:T(8,128)} %broadcast_in_dim.25), calls=%async_computation.3 | async-start | bytes 65536 | tf_op jit(solution)/shard_map/all_to_all | solution.py:428
  152.7 19.0 %all-to-all-start.4 = ((f32[128,4,8]{2,1,0:T(4,128)}), f32[128,4,8]{2,1,0:T(4,128)S(1)}, u32[]{:S(2)}, u32[]{:S(2)}) async-start(f32[128,4,8]{2,1,0:T(4,128)} %get-tuple-element.19), calls=%async_computation.4 | async-start | bytes 524288 | tf_op jit(solution)/shard_map/all_to_all | solution.py:437
  160.0 12.5 %collective-permute-start.1 = (bf16[4,64,256]{2,1,0:T(8,128)(2,1)}, bf16[4,64,256]{2,1,0:T(8,128)(2,1)S(1)}, u32[]{:S(2)}, u32[]{:S(2)}) collective-permute-start(bf16[4,64,256]{2,1,0:T(8,128)(2,1)} %get-tuple-element.15), channel_id=1, source_target_pairs={{0,0},{1,32},{32,64},{33,96},{64,1},{65,33},{96,65},{97,97},{2,2},... | collective-permute-start | bytes 393224 | tf_op jit(solution)/shard_map/ppermute | solution.py:446
  163.5 9.0 %collective-permute-start.2 = (bf16[4,64,256]{2,1,0:T(8,128)(2,1)}, bf16[4,64,256]{2,1,0:T(8,128)(2,1)S(1)}, u32[]{:S(2)}, u32[]{:S(2)}) collective-permute-start(bf16[4,64,256]{2,1,0:T(8,128)(2,1)} %get-tuple-element.16), channel_id=1, source_target_pairs={{0,32},{1,64},{32,96},{33,0},{64,33},{65,65},{96,97},{97,1},{2,34}... | collective-permute-start | bytes 393224 | tf_op jit(solution)/shard_map/ppermute | solution.py:446
  167.0 5.9 %collective-permute-start.3 = (bf16[4,64,256]{2,1,0:T(8,128)(2,1)}, bf16[4,64,256]{2,1,0:T(8,128)(2,1)S(1)}, u32[]{:S(2)}, u32[]{:S(2)}) collective-permute-start(bf16[4,64,256]{2,1,0:T(8,128)(2,1)} %get-tuple-element.17), channel_id=1, source_target_pairs={{0,64},{1,96},{32,0},{33,32},{64,65},{65,97},{96,1},{97,33},{2,66}... | collective-permute-start | bytes 393224 | tf_op jit(solution)/shard_map/ppermute | solution.py:446
  167.3 7.6 %collective-permute-start.4 = (bf16[4,64,256]{2,1,0:T(8,128)(2,1)}, bf16[4,64,256]{2,1,0:T(8,128)(2,1)S(1)}, u32[]{:S(2)}, u32[]{:S(2)}) collective-permute-start(bf16[4,64,256]{2,1,0:T(8,128)(2,1)} %get-tuple-element.18), channel_id=1, source_target_pairs={{0,96},{1,0},{32,32},{33,64},{64,97},{65,1},{96,33},{97,65},{2,98}... | collective-permute-start | bytes 393224 | tf_op jit(solution)/shard_map/ppermute | solution.py:446
Sparse Core Ops, SparseCore 0:
  11.0 121.0 all-gather.1
